TPU v7x, 32 devices: a whole 2x2x4 slice. The times are simulated.
32 devices in a mesh: dp: 8 (over y, x, core), tp: 4 (over z).
Axes of the slice: x: 2, y: 2, z: 4, core: 2. Of those that a mesh axis runs over, the one named last changes fastest.
Arguments:
- tokens: bfloat16 [4096, 768], P('dp'), may hold values from -6 to 6
- cotangent: bfloat16 [4096, 768], P('dp'), may hold values from -6 to 6
- norm1_gain: float32 [768], replicated, may hold values from 0.1 to 1.9
- w_input: bfloat16 [768, 768], P(None, 'tp'), may hold values from -0.21875 to 0.21875
- w_forget: bfloat16 [768, 384], P(None, 'tp'), may hold values from -0.21875 to 0.21875
- w_outgate: bfloat16 [768, 768], P(None, 'tp'), may hold values from -0.21875 to 0.21875
- forget_gap: float32 [384], P('tp'), may hold values from 0.0001 to 0.05
- phase_angle: float32 [384], P('tp'), may hold values from -3.140625 to 3.140625
- group_gain: float32 [768], P('tp'), may hold values from 0.1 to 1.9
- w_mix: bfloat16 [768, 768], P('tp'), may hold values from -0.21875 to 0.21875
- norm2_gain: float32 [768], replicated, may hold values from 0.1 to 1.9
- w_gate: bfloat16 [768, 1536], P(None, 'tp'), may hold values from -0.21875 to 0.21875
- w_up: bfloat16 [768, 1536], P(None, 'tp'), may hold values from -0.21875 to 0.21875
- w_down: bfloat16 [1536, 768], P('tp'), may hold values from -0.15625 to 0.15625
Outputs:
- mixed: bfloat16 [4096, 768], P('dp')
- token_grad: float32 [4096, 768], P('dp')
- grad_norm1: float32 [768], replicated
- grad_input: float32 [768, 768], P(None, 'tp')
- grad_forget: float32 [768, 384], P(None, 'tp')
- grad_outgate: float32 [768, 768], P(None, 'tp')
- grad_gap: float32 [384], P('tp')
- grad_phase: float32 [384], P('tp')
- grad_group: float32 [768], P('tp')
- grad_mix: float32 [768, 768], P('tp')
- grad_norm2: float32 [768], replicated
- grad_gate: float32 [768, 1536], P(None, 'tp')
- grad_up: float32 [768, 1536], P(None, 'tp')
- grad_down: float32 [1536, 768], P('tp')
All inputs are finite; a program needn't handle non-finite values.
Results may differ from a plain program's by a relative error of at most 0.0085.
The roundings to bfloat16 on the way count: a program that leaves them out, or rounds other values in their place, can miss the bound.
Values may be sent and summed in bfloat16 or wider, within the bound.
A program may use at most 128 MiB of HBM per device.

v0:
```python
import jax
import jax.numpy as jnp
from jax import lax
from jax.sharding import PartitionSpec as P

GROUP = 64


def prefix(shard, axis, combine, identity, reverse):
    size, mine = (lax.axis_size(axis), lax.axis_index(axis))
    everything = jax.tree.map(lambda part: lax.all_gather(part, axis), shard)
    start = jax.tree.map(
        lambda part, zero: jnp.broadcast_to(jnp.asarray(zero, part.dtype), part.shape),
        shard,
        identity,
    )

    def lap(k, before):
        at = size - 1 - k if reverse else k
        reached = at > mine if reverse else at < mine
        new = combine(before, jax.tree.map(lambda part: part[at], everything))
        return jax.tree.map(lambda a, b: jnp.where(reached, a, b), new, before)

    return lax.fori_loop(0, size, lap, start)


def product(left_side, right_side):
    return jnp.dot(left_side, right_side, preferred_element_type=jnp.float32)


def over_rows(left_side, right_side):
    return lax.dot_general(
        left_side, right_side, (((0,), (0,)), ((), ())), preferred_element_type=jnp.float32
    )


def over_cols(left_side, right_side):
    return lax.dot_general(
        left_side, right_side, (((1,), (1,)), ((), ())), preferred_element_type=jnp.float32
    )


def rms_norm(values, scales):
    return values * lax.rsqrt(jnp.mean(values * values, -1, keepdims=True) + 1e-06) * scales


def swish_product(gate_act, up_act):
    return jax.nn.silu(gate_act) * up_act


def combine(earlier, latter):
    return (
        latter[0] * earlier[0] - latter[1] * earlier[1],
        latter[0] * earlier[1] + latter[1] * earlier[0],
        latter[0] * earlier[2] - latter[1] * earlier[3] + latter[2],
        latter[0] * earlier[3] + latter[1] * earlier[2] + latter[3],
    )


def recurrence(in_real, in_imag, forget, forget_gap, phase_angle):
    leak_rate = forget_gap * jax.nn.sigmoid(-forget)
    retain = 1.0 - leak_rate
    return lax.associative_scan(
        combine,
        (
            retain * jnp.cos(phase_angle),
            retain * jnp.sin(phase_angle),
            leak_rate * jax.nn.silu(in_real),
            leak_rate * jax.nn.silu(in_imag),
        ),
        axis=0,
    )


def gated_norm(state_real, state_imag, gate_pre, group_gain):
    count_rows = state_real.shape[0]
    whole = jnp.stack([state_real, state_imag], -1).reshape(count_rows, -1)
    grouped = whole.reshape(count_rows, -1, GROUP)
    group_mean = jnp.mean(grouped, -1, keepdims=True)
    centered = grouped - group_mean
    group_var = jnp.mean(centered * centered, -1, keepdims=True)
    normed = (centered * lax.rsqrt(group_var + 1e-05)).reshape(count_rows, -1)
    return normed * group_gain * jax.nn.silu(gate_pre)


def local(
    tokens,
    cotangent,
    norm1_gain,
    w_input,
    w_forget,
    w_outgate,
    forget_gap,
    phase_angle,
    group_gain,
    w_mix,
    norm2_gain,
    w_gate,
    w_up,
    w_down,
):
    inputs = tokens.astype(jnp.float32)
    low_in = rms_norm(inputs, norm1_gain).astype(jnp.bfloat16)
    real_weight = w_input[:, 0::2]
    imag_weight = w_input[:, 1::2]
    in_real = product(low_in, real_weight)
    in_imag = product(low_in, imag_weight)
    forget = product(low_in, w_forget)
    gate_pre = product(low_in, w_outgate)
    scanned, pull_scan = jax.vjp(recurrence, in_real, in_imag, forget, forget_gap, phase_angle)
    decay_real, decay_imag, local_real, local_imag = scanned
    unit_row = jnp.ones_like(decay_real[-1])
    zero_row = jnp.zeros_like(decay_real[-1])
    before = prefix(
        (decay_real[-1], decay_imag[-1], local_real[-1], local_imag[-1]),
        "dp",
        combine,
        (unit_row, zero_row, zero_row, zero_row),
        False,
    )
    start_state = jnp.stack([before[2], before[3]])
    state_real = local_real + decay_real * start_state[0] - decay_imag * start_state[1]
    state_imag = local_imag + decay_real * start_state[1] + decay_imag * start_state[0]
    mix_act, pull_norm = jax.vjp(gated_norm, state_real, state_imag, gate_pre, group_gain)
    low_mix = mix_act.astype(jnp.bfloat16)
    grad_out = cotangent.astype(jnp.float32)
    resid = inputs + lax.psum(product(low_mix, w_mix), "tp")
    normed_mid, pull_second = jax.vjp(rms_norm, resid, norm2_gain)
    low_mid = normed_mid.astype(jnp.bfloat16)
    gate_act = product(low_mid, w_gate)
    up_act = product(low_mid, w_up)
    hidden_full, pull_swish = jax.vjp(swish_product, gate_act, up_act)
    hidden = hidden_full.astype(jnp.bfloat16)
    mixed = (resid + lax.psum(product(hidden, w_down), "tp")).astype(jnp.bfloat16)
    grad_down = over_rows(hidden, cotangent)
    grad_hidden = over_cols(cotangent, w_down)
    grad_gate_act, grad_up_act = pull_swish(grad_hidden)
    low_gate = grad_gate_act.astype(jnp.bfloat16)
    low_up = grad_up_act.astype(jnp.bfloat16)
    grad_gate = over_rows(low_mid, low_gate)
    grad_up = over_rows(low_mid, low_up)
    grad_mid = lax.psum(over_cols(low_gate, w_gate) + over_cols(low_up, w_up), "tp")
    grad_resid_norm, grad_norm2 = pull_second(grad_mid)
    grad_resid = grad_out + grad_resid_norm
    low_resid = grad_resid.astype(jnp.bfloat16)
    grad_mix = over_rows(low_mix, low_resid)
    grad_act = over_cols(low_resid, w_mix)
    grad_state_real, grad_state_imag, grad_gate_pre, grad_group = pull_norm(grad_act)
    start_real = jnp.sum(grad_state_real * decay_real + grad_state_imag * decay_imag, 0)
    start_imag = jnp.sum(grad_state_imag * decay_real - grad_state_real * decay_imag, 0)
    after = prefix(
        (decay_real[-1], -decay_imag[-1], start_real, start_imag),
        "dp",
        combine,
        (unit_row, zero_row, zero_row, zero_row),
        True,
    )
    grad_state_real = grad_state_real.at[-1].add(after[2])
    grad_state_imag = grad_state_imag.at[-1].add(after[3])
    grad_decay_real = grad_state_real * start_state[0] + grad_state_imag * start_state[1]
    grad_decay_imag = grad_state_imag * start_state[0] - grad_state_real * start_state[1]
    grad_in_real, grad_in_imag, grad_forget_act, grad_gap, grad_phase = pull_scan(
        (grad_decay_real, grad_decay_imag, grad_state_real, grad_state_imag)
    )
    low_real = grad_in_real.astype(jnp.bfloat16)
    low_imag = grad_in_imag.astype(jnp.bfloat16)
    low_forget = grad_forget_act.astype(jnp.bfloat16)
    low_gate_pre = grad_gate_pre.astype(jnp.bfloat16)
    grad_input = jnp.stack([over_rows(low_in, low_real), over_rows(low_in, low_imag)], -1).reshape(
        low_in.shape[1], -1
    )
    grad_forget = over_rows(low_in, low_forget)
    grad_outgate = over_rows(low_in, low_gate_pre)
    total = over_cols(low_real, real_weight) + over_cols(low_imag, imag_weight)
    grad_first = lax.psum(
        total + over_cols(low_forget, w_forget) + over_cols(low_gate_pre, w_outgate), "tp"
    )
    unused_normed, pull_first = jax.vjp(rms_norm, inputs, norm1_gain)
    grad_inputs, grad_norm1 = pull_first(grad_first)
    token_grad = grad_resid + grad_inputs
    summed = lax.psum(
        (
            grad_norm1,
            grad_input,
            grad_forget,
            grad_outgate,
            grad_gap,
            grad_phase,
            grad_group,
            grad_mix,
            grad_norm2,
            grad_gate,
            grad_up,
            grad_down,
        ),
        "dp",
    )
    return (
        mixed,
        token_grad,
        summed[0],
        summed[1],
        summed[2],
        summed[3],
        summed[4],
        summed[5],
        summed[6],
        summed[7],
        summed[8],
        summed[9],
        summed[10],
        summed[11],
    )


def solution(mesh):
    in_specs = (
        P("dp", None),
        P("dp", None),
        P(),
        P(None, "tp"),
        P(None, "tp"),
        P(None, "tp"),
        P("tp"),
        P("tp"),
        P("tp"),
        P("tp", None),
        P(),
        P(None, "tp"),
        P(None, "tp"),
        P("tp", None),
    )
    out_specs = (
        P("dp", None),
        P("dp", None),
        P(),
        P(None, "tp"),
        P(None, "tp"),
        P(None, "tp"),
        P("tp"),
        P("tp"),
        P("tp"),
        P("tp", None),
        P(),
        P(None, "tp"),
        P(None, "tp"),
        P("tp", None),
    )
    return jax.shard_map(local, mesh=mesh, in_specs=in_specs, out_specs=out_specs, check_vma=False)
```

profile of v0, /device:TPU:0, one launch (start us, length us, event | category | flops | bytes accessed | tf_op | source)
XLA Modules:
  0.0 648.6 jit_solution(12308182799403553598)
XLA Ops:
  59.0 11.2 %all-gather.4 = f32[8,1,96]{2,1,0:T(1,128)} all-gather(f32[1,1,96]{2,1,0:T(1,128)S(1)} %add_bitcast_fusion.1), channel_id=1, replica_groups=mesh['dp'=8,'tp'=4] {'dp'}, dimensions={0}, use_global_device_ids=true | all-gather | bytes 3456 | tf_op jit(solution)/shard_map/all_gather | solution.py:11
  72.2 9.7 %all-gather.2 = f32[8,1,96]{2,1,0:T(1,128)} all-gather(f32[1,1,96]{2,1,0:T(1,128)S(1)} %add_bitcast_fusion.2), channel_id=1, replica_groups=mesh['dp'=8,'tp'=4] {'dp'}, dimensions={0}, use_global_device_ids=true | all-gather | bytes 3456 | tf_op jit(solution)/shard_map/all_gather | solution.py:11
  84.4 7.8 %all-gather.5 = f32[8,1,96]{2,1,0:T(1,128)S(1)} all-gather(f32[1,1,96]{2,1,0:T(1,128)S(1)} %add_bitcast_fusion), channel_id=1, replica_groups=mesh['dp'=8,'tp'=4] {'dp'}, dimensions={0}, use_global_device_ids=true | all-gather | bytes 3456 | tf_op jit(solution)/shard_map/all_gather | solution.py:11
  93.7 8.7 %all-gather.3 = f32[8,1,96]{2,1,0:T(1,128)S(1)} all-gather(f32[1,1,96]{2,1,0:T(1,128)S(1)} %get-tuple-element.606), channel_id=1, replica_groups=mesh['dp'=8,'tp'=4] {'dp'}, dimensions={0}, use_global_device_ids=true | all-gather | bytes 3456 | tf_op jit(solution)/shard_map/all_gather | solution.py:11
  102.4 5.7 while.36
  108.7 2.2 fusion.65
  112.3 2.3 multiply_convert_fusion.3
  116.3 69.3 %all-reduce.251.cloned.1.call-done = f32[512,768]{1,0:T(8,128)} async-done(((f32[512,768]{1,0:T(8,128)}), f32[512,768]{1,0:T(8,128)}) %all-reduce.251.cloned.1.call-update) | async-done | bytes 1572880 | tf_op jit(solution)/shard_map/psum | solution.py:127
  198.6 9.7 %all-gather.6 = f32[8,1,96]{2,1,0:T(1,128)} all-gather(f32[1,1,96]{2,1,0:T(1,128)S(1)} %copy-done.260), channel_id=1, replica_groups=mesh['dp'=8,'tp'=4] {'dp'}, dimensions={0}, use_global_device_ids=true | all-gather | bytes 3456 | tf_op jit(solution)/shard_map/all_gather | solution.py:11
  208.3 2.7 fusion.104
  211.0 52.7 %all-reduce.253.cloned.1.call-done = f32[512,768]{1,0:T(8,128)} async-done(((f32[512,768]{1,0:T(8,128)}), f32[512,768]{1,0:T(8,128)}) %all-reduce.253.cloned.1.call-update) | async-done | bytes 1572880 | tf_op jit(solution)/shard_map/psum | solution.py:142
  263.7 2.6 multiply_reduce_fusion
  274.9 12.7 %all-reduce.243 = (f32[768]{0:T(1024)S(1)}, f32[768]{0:T(1024)S(1)}) all-reduce(f32[768]{0:T(1024)S(1)} %dynamic-update-slice.6, f32[768]{0:T(1024)S(1)} %dynamic-update-slice.7), channel_id=2, replica_groups=mesh['dp'=8,'tp'=4] {'dp'}, use_global_device_ids=true, to_apply=%add.240 | all-reduce | flops 1536 | bytes 12288
  287.7 5.8 while.37
  361.9 2.2 pad.1332
  366.2 2.2 pad.1214
  372.4 2.2 pad.1231
  374.7 2.2 pad.1108
  384.6 2.4 pad.1215
  386.9 2.4 pad.1334
  389.3 2.3 pad.1219
  391.7 2.4 pad.1338
  394.0 2.4 pad.1335
  396.4 2.4 pad.1339
  398.8 2.4 pad.1223
  401.1 2.4 pad.1102
  403.6 2.6 multiply_reduce_fusion.7
  411.0 2.8 fusion.111
  424.4 105.8 %all-reduce.257.cloned.1.call-done = (f32[512,768]{1,0:T(8,128)}, f32[512,768]{1,0:T(8,128)}) async-done(((f32[512,768]{1,0:T(8,128)}, f32[512,768]{1,0:T(8,128)}), (f32[512,768]{1,0:T(8,128)}, f32[512,768]{1,0:T(8,128)})) %all-reduce.257.cloned.1.call-update) | async-done | bytes 3145744 | tf_op jit(solution)/shard_map/psum | solution.py:134
  532.2 25.1 %all-reduce.242 = (f32[768]{0:T(1024)}, f32[96]{0:T(128)}, f32[96]{0:T(128)}, f32[192]{0:T(256)}, f32[768]{0:T(1024)}) all-reduce(f32[768]{0:T(1024)S(1)} %get-tuple-element.437, f32[96]{0:T(128)S(1)} %get-tuple-element.443, f32[96]{0:T(128)S(1)} %multiply_add_fusion.110, ...), channel_id=1, replica_groups=mesh['dp'=8,'tp'=4] {'dp'}, use_global_device_ids=true, to_apply=%region_20.21 | all-reduce | flops 1920 | bytes 15360 | tf_op jit(solution)/shard_map/psum | solution.py:181
  557.3 2.6 add_convert_fusion
  561.5 71.4 %all-reduce.255.cloned.1.call-done = (f32[768,192]{0,1:T(8,128)}, f32[768,96]{0,1:T(8,128)}, f32[768,192]{0,1:T(8,128)}, f32[192,768]{1,0:T(8,128)}, f32[768,384...) async-done(((f32[768,192]{0,1:T(8,128)}, f32[768,96]{0,1:T(8,128)}, f32[768,192]{0,1:T(8,128)}, f32[192,768]{1,0:T(8,128)}, f32[768,384]{1,0:T(8,128)}, ...) | async-done | bytes 5603344 | tf_op jit(solution)/shard_map/psum | solution.py:181
  (1229 shorter events, 198.9 us)
Async XLA Ops:
  7.2 183.4 %copy-start = (bf16[384,768]{1,0:T(8,128)(2,1)S(1)}, bf16[384,768]{1,0:T(8,128)(2,1)}, u32[]{:S(2)}) copy-start(bf16[384,768]{1,0:T(8,128)(2,1)} %param.35) | copy-start | bytes 1769476
  7.2 178.4 %all-reduce.251.cloned.1.call-start = ((), (), s32[]{:S(2)}) async-start(), calls=%async_computation | async-start | bytes 3145728 | tf_op jit(solution)/shard_map/psum | solution.py:127
  17.2 65.7 %copy-start.12 = (f32[255,96]{1,0:T(8,128)}, f32[255,96]{1,0:T(8,128)S(1)}, u32[]{:S(2)}) copy-start(f32[255,96]{1,0:T(8,128)S(1)} %slice.846) | copy-start | bytes 293764
  18.0 64.9 %copy-start.14 = (f32[255,96]{1,0:T(8,128)}, f32[255,96]{1,0:T(8,128)S(1)}, u32[]{:S(2)}) copy-start(f32[255,96]{1,0:T(8,128)S(1)} %slice.973) | copy-start | bytes 293764
  23.1 30.6 %copy-start.28 = (f32[127,96]{1,0:T(8,128)}, f32[127,96]{1,0:T(8,128)S(1)}, u32[]{:S(2)}) copy-start(f32[127,96]{1,0:T(8,128)S(1)} %slice.856) | copy-start | bytes 146308
  24.5 28.1 %copy-start.69 = (f32[63,96]{1,0:T(8,128)}, f32[63,96]{1,0:T(8,128)S(1)}, u32[]{:S(2)}) copy-start(f32[63,96]{1,0:T(8,128)S(1)} %slice.961) | copy-start | bytes 72580
  24.6 28.1 %copy-start.71 = (f32[63,96]{1,0:T(8,128)}, f32[63,96]{1,0:T(8,128)S(1)}, u32[]{:S(2)}) copy-start(f32[63,96]{1,0:T(8,128)S(1)} %slice.866) | copy-start | bytes 72580
  24.6 26.0 %copy-start.122 = (f32[64,96]{1,0:T(8,128)}, f32[64,96]{1,0:T(8,128)S(1)}, u32[]{:S(2)}) copy-start(f32[64,96]{1,0:T(8,128)S(1)} %slice.871) | copy-start | bytes 73732
  24.7 26.0 %copy-start.124 = (f32[64,96]{1,0:T(8,128)}, f32[64,96]{1,0:T(8,128)S(1)}, u32[]{:S(2)}) copy-start(f32[64,96]{1,0:T(8,128)S(1)} %slice.868) | copy-start | bytes 73732
  24.7 26.4 %copy-start.126 = (f32[64,96]{1,0:T(8,128)}, f32[64,96]{1,0:T(8,128)S(1)}, u32[]{:S(2)}) copy-start(f32[64,96]{1,0:T(8,128)S(1)} %slice.875) | copy-start | bytes 73732
  24.7 26.4 %copy-start.114 = (f32[64,96]{1,0:T(8,128)}, f32[64,96]{1,0:T(8,128)S(1)}, u32[]{:S(2)}) copy-start(f32[64,96]{1,0:T(8,128)S(1)} %slice.869) | copy-start | bytes 73732
  24.8 26.3 %copy-start.128 = (f32[64,96]{1,0:T(8,128)}, f32[64,96]{1,0:T(8,128)S(1)}, u32[]{:S(2)}) copy-start(f32[64,96]{1,0:T(8,128)S(1)} %slice.874) | copy-start | bytes 73732
  24.8 26.4 %copy-start.116 = (f32[64,96]{1,0:T(8,128)}, f32[64,96]{1,0:T(8,128)S(1)}, u32[]{:S(2)}) copy-start(f32[64,96]{1,0:T(8,128)S(1)} %slice.867) | copy-start | bytes 73732
  25.0 26.4 %copy-start.131 = (f32[31,96]{1,0:T(8,128)}, f32[31,96]{1,0:T(8,128)S(1)}, u32[]{:S(2)}) copy-start(f32[31,96]{1,0:T(8,128)S(1)} %slice.876) | copy-start | bytes 35716
  25.0 26.3 %copy-start.156 = (f32[32,96]{1,0:T(8,128)}, f32[32,96]{1,0:T(8,128)S(1)}, u32[]{:S(2)}) copy-start(f32[32,96]{1,0:T(8,128)S(1)} %slice.881) | copy-start | bytes 36868
  25.1 26.3 %copy-start.158 = (f32[32,96]{1,0:T(8,128)}, f32[32,96]{1,0:T(8,128)S(1)}, u32[]{:S(2)}) copy-start(f32[32,96]{1,0:T(8,128)S(1)} %slice.878) | copy-start | bytes 36868
  25.1 26.3 %copy-start.160 = (f32[32,96]{1,0:T(8,128)}, f32[32,96]{1,0:T(8,128)S(1)}, u32[]{:S(2)}) copy-start(f32[32,96]{1,0:T(8,128)S(1)} %slice.885) | copy-start | bytes 36868
  25.1 26.2 %copy-start.150 = (f32[32,96]{1,0:T(8,128)}, f32[32,96]{1,0:T(8,128)S(1)}, u32[]{:S(2)}) copy-start(f32[32,96]{1,0:T(8,128)S(1)} %slice.879) | copy-start | bytes 36868
  25.2 26.2 %copy-start.152 = (f32[32,96]{1,0:T(8,128)}, f32[32,96]{1,0:T(8,128)S(1)}, u32[]{:S(2)}) copy-start(f32[32,96]{1,0:T(8,128)S(1)} %slice.877) | copy-start | bytes 36868
  25.3 26.6 %copy-start.166 = (f32[15,96]{1,0:T(8,128)}, f32[15,96]{1,0:T(8,128)S(1)}, u32[]{:S(2)}) copy-start(f32[15,96]{1,0:T(8,128)S(1)} %slice.949) | copy-start | bytes 17284
  25.4 26.5 %copy-start.168 = (f32[15,96]{1,0:T(8,128)}, f32[15,96]{1,0:T(8,128)S(1)}, u32[]{:S(2)}) copy-start(f32[15,96]{1,0:T(8,128)S(1)} %slice.886) | copy-start | bytes 17284
  58.1 26.2 %copy-start.92 = (f32[512,96]{1,0:T(8,128)}, f32[512,96]{1,0:T(8,128)S(1)}, u32[]{:S(2)}) copy-start(f32[512,96]{1,0:T(8,128)S(1)} %pad.1060) | copy-start | bytes 589828
  116.1 71.5 %copy-start.230 = (f32[768]{0:T(1024)S(1)}, f32[768]{0:T(1024)}, u32[]{:S(2)}) copy-start(f32[768]{0:T(1024)} %param.32) | copy-start | bytes 9220
  116.1 147.6 %all-reduce.253.cloned.1.call-start = ((), (), s32[]{:S(2)}) async-start(), calls=%async_computation.1 | async-start | bytes 3145728 | tf_op jit(solution)/shard_map/psum | solution.py:142
  195.4 334.8 %all-reduce.257.cloned.1.call-start = ((), (), s32[]{:S(2)}) async-start(), calls=%async_computation.3 | async-start | bytes 6291456 | tf_op jit(solution)/shard_map/psum | solution.py:134
  410.1 222.8 %all-reduce.255.cloned.1.call-start = ((), (), s32[]{:S(2)}) async-start(), calls=%async_computation.2 | async-start | bytes 11206656 | tf_op jit(solution)/shard_map/psum | solution.py:181
  423.7 106.5 %copy-start.3 = (bf16[512,768]{1,0:T(8,128)(2,1)S(1)}, bf16[512,768]{1,0:T(8,128)(2,1)}, u32[]{:S(2)}) copy-start(bf16[512,768]{1,0:T(8,128)(2,1)} %param.22) | copy-start | bytes 2359300
  423.7 106.5 %copy-start.231 = (f32[768]{0:T(1024)S(1)}, f32[768]{0:T(1024)}, u32[]{:S(2)}) copy-start(f32[768]{0:T(1024)} %param.24) | copy-start | bytes 9220
  423.7 106.5 %copy-start.233 = (f32[512]{0:T(512)S(1)}, f32[512]{0:T(512)}, u32[]{:S(2)}) copy-start(f32[512]{0:T(512)} %copy-done.232) | copy-start | bytes 6148
  423.8 108.4 %copy-start.246 = (f32[768]{0:T(1024)S(1)}, f32[768]{0:T(1024)}, u32[]{:S(2)}) copy-start(f32[768]{0:T(1024)} %get-tuple-element.435) | copy-start | bytes 9220
  423.8 108.4 %copy-start.262 = (f32[192]{0:T(256)S(1)}, f32[192]{0:T(256)}, u32[]{:S(2)}) copy-start(f32[192]{0:T(256)} %get-tuple-element.586) | copy-start | bytes 2308
  423.8 133.5 %copy-start.243 = (f32[512]{0:T(512)S(1)}, f32[512]{0:T(512)}, u32[]{:S(2)}) copy-start(f32[512]{0:T(512)} %copy-done.242) | copy-start | bytes 6148
  (257 other events, 2056.2 us)
Sparse Core Ops, SparseCore 0:
  116.2 69.3 all-reduce.250
  195.5 68.1 all-reduce.252
  410.2 119.9 all-reduce.256
  535.4 97.3 all-reduce.254
where the time goes:
time: 652 us; the launch traced here: 649 us
  waiting for transfers between devices  299 us (46%)
  local copies, waits for them, and re-layouts  136 us (21%)
  blocking collectives  84.8 us (13%)
  other arithmetic  78.9 us (12%)
  matrix products  28.9 us (4%)
  between operations  20 us (3%)
    psum x1, waiting for transfers between devices, local(): lax.psum(product(hidden, w_down), 'tp')  106 us
    psum x1, waiting for transfers between devices, local(): lax.psum((grad_norm1, grad_input, grad_forget, grad_outgate, grad_gap, gr...  71.4 us
    pad x188, local copies, waits for them, and re-layouts, recurrence(): lax.associative_scan(combine, (retain * jnp.cos(phase_angle), retain * jn...  71.1 us
    psum x1, waiting for transfers between devices, local(): resid = inputs + lax.psum(product(low_mix, w_mix), 'tp')  69.3 us
    psum x1, waiting for transfers between devices, local(): lax.psum(over_cols(low_gate, w_gate) + over_cols(low_up, w_up), 'tp')  52.7 us
    all_gather x5, blocking collectives, prefix(): everything = jax.tree.map(lambda part: lax.all_gather(part, axis), shard)  47 us
    slice x190, local copies, waits for them, and re-layouts, recurrence(): lax.associative_scan(combine, (retain * jnp.cos(phase_angle), retain * jn...  29.8 us
    psum x1, blocking collectives, local(): lax.psum((grad_norm1, grad_input, grad_forget, grad_outgate, grad_gap, gr...  25.1 us
  transfers between devices with their start and end apart: 4, of which 4 were waited for; matrix products, arithmetic and copies ran while one was open for 4% of the time, Pallas kernels for 0%

commit v1 on v0

v1 whole, which is shorter than its diff:
```python
import functools

import jax
import jax.numpy as jnp
from jax import lax
from jax.experimental import pallas as pl
from jax.experimental.pallas import tpu as pltpu
from jax.sharding import PartitionSpec as P

MESH = pl.DeviceIdType.MESH
BF = jnp.bfloat16
F32 = jnp.float32
GROUP = 64
LANES = 128


def nn(a, b):
    return jnp.dot(a, b, preferred_element_type=F32)


def nt(a, b):
    return lax.dot_general(a, b, (((1,), (1,)), ((), ())), preferred_element_type=F32)


def tn(a, b):
    return lax.dot_general(a, b, (((0,), (0,)), ((), ())), preferred_element_type=F32)


def cells(shape, axis):
    return lax.broadcasted_iota(jnp.int32, shape, axis)


def one_hot(flags):
    return jnp.where(flags, 1.0, 0.0).astype(BF)


def down_sum(v):
    if v.shape[0] > 8:
        v = jnp.sum(v.reshape(v.shape[0] // 8, 8, v.shape[1]), 0)
    v = v[0:4] + v[4:8]
    v = v[0:2] + v[2:4]
    return v[0:1] + v[1:2]


def power(c, s, n):
    out = None
    while n:
        if n % 2:
            out = (c, s) if out is None else (out[0] * c - out[1] * s, out[0] * s + out[1] * c)
        c, s = c * c - s * s, 2.0 * c * s
        n //= 2
    return out


def scratch_list(nd, nt_, T):
    dma = pltpu.SemaphoreType.DMA
    return dict(
        WI=pltpu.VMEM((2, 8, nt_, 64, 384), BF),
        WX=pltpu.VMEM((2, 4, nt_, 48, 384), BF),
        WM=pltpu.VMEM((2, 8, nt_, 144, 384), BF),
        PAR=pltpu.VMEM((nt_, 8, LANES), F32),
        WRP=pltpu.VMEM((nt_, 640, 768), BF),
        WXP=pltpu.VMEM((nt_, 256, 768), BF),
        NAT=pltpu.VMEM((T, 768), F32),
        PERM=pltpu.VMEM((6, T, LANES), F32),
        X=pltpu.VMEM((T, 768), F32),
        GY=pltpu.VMEM((T, 768), BF),
        LOW=pltpu.VMEM((T, 768), BF),
        ACT=pltpu.VMEM((nt_, T, 640), F32),
        LAM=pltpu.VMEM((nt_, T, LANES), F32),
        BR=pltpu.VMEM((nt_, T, LANES), F32),
        BI=pltpu.VMEM((nt_, T, LANES), F32),
        HR=pltpu.VMEM((nt_, T + 8, LANES), F32),
        HI=pltpu.VMEM((nt_, T + 8, LANES), F32),
        NR=pltpu.VMEM((nt_, T, LANES), F32),
        NI=pltpu.VMEM((nt_, T, LANES), F32),
        RS=pltpu.VMEM((nt_, T, LANES), F32),
        MIX=pltpu.VMEM((nt_, T, 256), BF),
        RES=pltpu.VMEM((T, 768), F32),
        MID=pltpu.VMEM((T, 768), BF),
        GRES0=pltpu.VMEM((T, 768), BF),
        HID=pltpu.VMEM((nt_, T, 384), BF),
        DG=pltpu.VMEM((nt_, T, 768), BF),
        GRES=pltpu.VMEM((T, 768), F32),
        CH=pltpu.VMEM((3, nt_ * 8, LANES), F32),
        ST=pltpu.VMEM((2, nt_ * 8, LANES), F32),
        EXF=pltpu.VMEM((nd, 16, LANES), F32),
        EXB=pltpu.VMEM((nd, 16, LANES), F32),
        EXV=pltpu.VMEM((nd, 16, LANES), F32),
        SM=pltpu.VMEM((2, 8, 144, 384), BF),
        SM0=pltpu.VMEM((2, 4, 144, 384), BF),
        SM1=pltpu.VMEM((2, 2, 144, 384), BF),
        SM2=pltpu.VMEM((2, 1, 144, 384), BF),
        SME=pltpu.VMEM((2, max(1, nd.bit_length() - 4), 144, 384), BF),
        SMF=pltpu.VMEM((2, 8, 144, 384), BF),
        SI=pltpu.VMEM((2, 8, 48, 512), BF),
        SI0=pltpu.VMEM((2, 4, 48, 512), BF),
        SI1=pltpu.VMEM((2, 2, 48, 512), BF),
        SI2=pltpu.VMEM((2, 1, 48, 512), BF),
        SIE=pltpu.VMEM((2, max(1, nd.bit_length() - 4), 48, 512), BF),
        SIF=pltpu.VMEM((2, 8, 48, 512), BF),
        SX=pltpu.VMEM((2, 8, 32, 384), BF),
        SX0=pltpu.VMEM((2, 4, 32, 384), BF),
        SX1=pltpu.VMEM((2, 2, 32, 384), BF),
        SX2=pltpu.VMEM((2, 1, 32, 384), BF),
        SXE=pltpu.VMEM((2, max(1, nd.bit_length() - 4), 32, 384), BF),
        SXF=pltpu.VMEM((2, 8, 32, 384), BF),
        loc=dma((8,)),
        out=dma((8,)),
        ss=dma((160,)),
        rs=dma((160,)),
        es=dma((3, nd)),
        er=dma((3, nd)),
    )


class Links:
    def __init__(self, ss, rs):
        self.ss, self.rs, self.used, self.open = ss, rs, 0, []

    def send(self, src, dst, dev):
        k = self.used
        self.used += 1
        copy = pltpu.make_async_remote_copy(
            src, dst, self.ss.at[k], self.rs.at[k], device_id=dev, device_id_type=MESH
        )
        copy.start()
        self.open.append(copy)
        return copy

    def drain(self):
        for copy in self.open:
            copy.wait_send()
        self.open = []


def kernel(nd, nt_, T, names, *refs):
    r = dict(zip(names, refs))
    me, z = lax.axis_index("dp"), lax.axis_index("tp")
    steps = T // 8
    ch = r["gap"].shape[1]

    def flip(bit):
        return me + bit - 2 * bit * ((me // bit) % 2)

    bits = (me % 2, (me // 2) % 2, (me // 4) % 2)
    order = ((1, 2), (2, 1))
    place = [bits[0] * 4 + bits[f] * 2 + bits[s] for f, s in order]
    wide = [bits[0] * 2 + bits[f] for f, s in order]
    links = Links(r["ss"], r["rs"])

    WM = r["WM"]
    loads = [
        pltpu.make_async_copy(r["wg"], WM.at[0, :, 0, 0:96, :], r["loc"].at[0]),
        pltpu.make_async_copy(r["wu"], WM.at[1, :, 0, 0:96, :], r["loc"].at[1]),
        pltpu.make_async_copy(r["wd"].at[:, :, 0:384], WM.at[0, :, 0, 96:144, :], r["loc"].at[2]),
        pltpu.make_async_copy(r["wd"].at[:, :, 384:768], WM.at[1, :, 0, 96:144, :], r["loc"].at[3]),
    ]
    loads_in = [
        pltpu.make_async_copy(r["tokens"], r["MID"], r["loc"].at[4]),
        pltpu.make_async_copy(r["cot"], r["GRES0"], r["loc"].at[5]),
    ]
    for copy in loads_in + loads:
        copy.start()

    barrier = pltpu.get_barrier_semaphore()

    def greet_dp(o, c):
        pl.semaphore_signal(barrier, 1, device_id=(lax.rem(me + o, nd), z), device_id_type=MESH)
        return c

    def greet_tp(o, c):
        pl.semaphore_signal(barrier, 1, device_id=(me, lax.rem(z + o, nt_)), device_id_type=MESH)
        return c

    lax.fori_loop(1, nd, greet_dp, 0)
    lax.fori_loop(1, nt_, greet_tp, 0)

    WI, WX, WRP, WXP, PAR = r["WI"], r["WX"], r["WRP"], r["WXP"], r["PAR"]
    rows, cols = cells((2 * ch, 2 * ch), 0), cells((2 * ch, 2 * ch), 1)
    apart = one_hot(cols == jnp.where(rows < ch, 2 * rows, 2 * (rows - ch) + 1))
    eye = one_hot(cells((ch, ch), 0) == cells((ch, ch), 1))
    turned = jnp.concatenate(
        [
            nt(apart, r["w_in"][...]).astype(BF),
            nt(eye, r["w_f"][...]).astype(BF),
            nt(apart, r["w_o"][...]).astype(BF),
            jnp.zeros((32, 768), BF),
        ],
        axis=0,
    )
    mixed_rows = nn(apart, r["w_mix"][...]).astype(BF)
    for h in range(2):
        for p in range(8):
            WI[h, p, 0] = turned[64 * p : 64 * p + 64, 384 * h : 384 * h + 384]
        for p in range(4):
            WX[h, p, 0] = mixed_rows[48 * p : 48 * p + 48, 384 * h : 384 * h + 384]
    PAR[0] = jnp.zeros((8, LANES), F32)
    PAR[0, 0:1, 0:ch] = r["gap"][...]
    PAR[0, 1:2, 0:ch] = r["phase"][...]
    gains = lax.dot_general(
        jnp.broadcast_to(r["gg"][...], (8, 2 * ch)),
        apart.astype(F32),
        (((1,), (1,)), ((), ())),
        precision=lax.Precision.HIGHEST,
        preferred_element_type=F32,
    )
    PAR[0, 2:3, 0:ch] = gains[0:1, 0:ch]
    PAR[0, 3:4, 0:ch] = gains[0:1, ch : 2 * ch]

    for k in range(nt_):
        for g in range(5):
            WRP[k, g * 128 + 96 : g * 128 + 128, :] = jnp.zeros((32, 768), BF)
        for g in range(2):
            WXP[k, g * 128 + 96 : g * 128 + 128, :] = jnp.zeros((32, 768), BF)

    def spread_in(k):
        for g in range(5):
            for q in range(3):
                row = g * 96 + q * 32
                for h in range(2):
                    WRP[k, g * 128 + q * 32 : g * 128 + q * 32 + 32, 384 * h : 384 * h + 384] = WI[
                        h, row // 64, k, row % 64 : row % 64 + 32, :
                    ]

    def spread_mix(k):
        for p in range(4):
            row = (p // 2) * 128 + (p % 2) * 48
            for h in range(2):
                WXP[k, row : row + 48, 384 * h : 384 * h + 384] = WX[h, p, k]

    pl.semaphore_wait(barrier, nd - 1 + nt_ - 1)

    def across(o):
        return (me, lax.rem(z + nt_ - o, nt_))

    def partner(b):
        return (flip(1 << b), z)

    class Unit:
        def __init__(self, buf, slots, portions):
            self.buf, self.slots, self.portions = buf, slots, portions
            self.todo = []

        def view(self, h, start, count):
            return self.buf.at[h, pl.ds(start, count), pl.ds(self.slots[0], len(self.slots))]

        def stage(self, n):
            for copy in self.todo:
                copy.wait_recv()
            self.todo = []
            if n == 0:
                for h in range(2):
                    at = place[h] if self.portions == 8 else wide[h]
                    for o in self.slots:
                        self.todo.append(
                            links.send(self.buf.at[h, at, 0], self.buf.at[h, at, o], across(o))
                        )
            elif n in (1, 2, 3):
                for h in range(2):
                    f, s = order[h]
                    if self.portions == 8:
                        b, start, count = (
                            (s, place[h], 1),
                            (f, bits[0] * 4 + bits[f] * 2, 2),
                            (0, bits[0] * 4, 4),
                        )[n - 1]
                    else:
                        if n == 2:
                            continue
                        b, start, count = ((f, wide[h], 1), None, (0, bits[0] * 2, 2))[n - 1]
                    part = self.view(h, start, count)
                    self.todo.append(links.send(part, part, partner(b)))

    others = list(range(1, nt_))
    units = [Unit(WI, others, 8), Unit(WX, others, 4)] + [Unit(WM, [o], 8) for o in others]

    def gather_round(n):
        for u, unit in enumerate(units):
            if 0 <= n - u <= 4:
                unit.stage(n - u)

    par_copies = [links.send(PAR.at[0], PAR.at[o], across(o)) for o in others]
    gather_round(0)

    NAT, X, GY, LOW = r["NAT"], r["X"], r["GY"], r["LOW"]
    PERM = r["PERM"]
    for copy in loads_in:
        copy.wait()
    tiles = [slice(LANES * i, LANES * i + LANES) for i in range(6)]
    for i in range(6):
        PERM[i] = r["MID"][:, tiles[i]].astype(F32)

    def take(k, c):
        for i in range(6):
            X[pl.ds(pl.multiple_of(8 * k, 8), 8), tiles[i]] = PERM[i, pl.ds(k, 8, stride=steps), :]
        return c

    lax.fori_loop(0, steps, take, 0, unroll=4)
    def norm_rows(src, gain, dst):
        def body(i, c):
            at = pl.ds(pl.multiple_of(i * 128, 128), 128)
            v = src[at, :]
            q = lax.rsqrt(jnp.mean(v * v, -1, keepdims=True) + 1e-06)
            dst[at, :] = (v * q * gain[...]).astype(BF)
            return c

        lax.fori_loop(0, T // 128, body, 0)

    norm_rows(X, r["g1"], LOW)
    for i in range(6):
        PERM[i] = r["GRES0"][:, tiles[i]].astype(F32)

    def take_cot(k, c):
        for i in range(6):
            two = [PERM[i, pl.ds(2 * k + j, 8, stride=steps), :] for j in range(2)]
            GY[pl.ds(pl.multiple_of(16 * k, 16), 16), tiles[i]] = jnp.concatenate(two, axis=0).astype(BF)
        return c

    lax.fori_loop(0, steps // 2, take_cot, 0, unroll=2)

    ACT, LAM, BR, BI = r["ACT"], r["LAM"], r["BR"], r["BI"]

    def project(k):
        gap = PAR[k, 0:1, :]
        ACT[k] = nt(LOW[...], WRP[k])
        ur, ui, fg = ACT[k, :, 0:128], ACT[k, :, 128:256], ACT[k, :, 256:384]
        leak = gap * jax.nn.sigmoid(-fg)
        LAM[k] = 1.0 - leak
        BR[k] = leak * (ur * jax.nn.sigmoid(ur))
        BI[k] = leak * (ui * jax.nn.sigmoid(ui))

    spread_in(0)
    spread_mix(0)
    project(0)
    for copy in loads:
        copy.wait()
    for n in range(1, 4):
        gather_round(n)
    for copy in par_copies:
        copy.wait_recv()
    gather_round(4)

    def project_other(k, c):
        spread_in(k)
        project(k)
        return c

    lax.fori_loop(1, nt_, project_other, 0)

    CH, ST, HR, HI = r["CH"], r["ST"], r["HR"], r["HI"]
    turn = []
    for k in range(nt_):
        ph = PAR[k, 1:2, :]
        turn.append((jnp.cos(ph), jnp.sin(ph)))
    turn8 = [(jnp.broadcast_to(c, (8, LANES)), jnp.broadcast_to(s, (8, LANES))) for c, s in turn]
    cos4 = jnp.concatenate([c for c, s in turn], axis=0)
    sin4 = jnp.concatenate([s for c, s in turn], axis=0)
    chunk_c, chunk_s = power(cos4, sin4, steps)
    whole_c, whole_s = power(cos4, sin4, T)
    zero8 = jnp.zeros((8, LANES), F32)
    zero4 = jnp.zeros((nt_, LANES), F32)

    def rows_of(k):
        return pl.ds(pl.multiple_of(8 * k, 8), 8)

    def ends(n, carry):
        out = []
        for k in range(nt_):
            hr, hi, lp = carry[k]
            c, s = turn8[k]
            lam = LAM[k, rows_of(n), :]
            nr = lam * (c * hr - s * hi) + BR[k, rows_of(n), :]
            ni = lam * (c * hi + s * hr) + BI[k, rows_of(n), :]
            out.append((nr, ni, lp * lam))
        return tuple(out)

    last = lax.fori_loop(
        0, steps, ends, tuple((zero8, zero8, zero8 + 1.0) for k in range(nt_)), unroll=4
    )
    for k in range(nt_):
        CH[0, 8 * k : 8 * k + 8, :] = last[k][2]
        CH[1, 8 * k : 8 * k + 8, :] = last[k][0]
        CH[2, 8 * k : 8 * k + 8, :] = last[k][1]

    def chunk(i, c):
        return CH[i, pl.ds(c, nt_, stride=8), :]

    def chain(sr, si, sign, keep):
        for c in range(8) if sign > 0 else range(7, -1, -1):
            if keep:
                ST[0, pl.ds(c, nt_, stride=8), :] = sr
                ST[1, pl.ds(c, nt_, stride=8), :] = si
            lp = chunk(0, c)
            pr, pi = lp * chunk_c, sign * (lp * chunk_s)
            sr, si = pr * sr - pi * si + chunk(1, c), pr * si + pi * sr + chunk(2, c)
        return sr, si

    whole_lam = chunk(0, 0)
    for c in range(1, 8):
        whole_lam = whole_lam * chunk(0, c)

    def exchange(which, buf, start):
        def copy_to(o):
            at = lax.rem(me + o, nd)
            return pltpu.make_async_remote_copy(
                buf.at[me],
                buf.at[me],
                r["es"].at[which, o],
                r["er"].at[which, o],
                device_id=(at, z),
                device_id_type=MESH,
            )

        def wait_from(o):
            at = lax.rem(me + nd - o, nd)
            return pltpu.make_async_remote_copy(
                buf.at[at],
                buf.at[at],
                r["es"].at[which, o],
                r["er"].at[which, o],
                device_id=(at, z),
                device_id_type=MESH,
            )

        def go(o, c):
            copy_to(o).start()
            return c

        def arrive(o, c):
            wait_from(o).wait_recv()
            return c

        def leave(o, c):
            copy_to(o).wait_send()
            return c

        lax.fori_loop(1, nd, {"go": go, "arrive": arrive, "leave": leave}[start], 0)

    def post(buf, which, sr, si):
        buf[me, 0:4, :] = whole_lam
        buf[me, 4:8, :] = sr
        buf[me, 8:12, :] = si
        buf[me, 12:16, :] = zero4
        exchange(which, buf, "go")

    def carried(buf, which, sign):
        exchange(which, buf, "arrive")

        def lap(k, s):
            at = k if sign > 0 else nd - 1 - k
            reached = (at < me) if sign > 0 else (at > me)
            lp = buf[at, 0:4, :]
            pr, pi = lp * whole_c, sign * (lp * whole_s)
            nr = pr * s[0] - pi * s[1] + buf[at, 4:8, :]
            ni = pr * s[1] + pi * s[0] + buf[at, 8:12, :]
            return jnp.where(reached, nr, s[0]), jnp.where(reached, ni, s[1])

        return lax.fori_loop(0, nd, lap, (zero4, zero4))

    post(r["EXF"], 0, *chain(zero4, zero4, 1.0, False))
    gather_round(5)
    lax.fori_loop(1, nt_, lambda k, c: (spread_mix(k), c)[1], 0)
    start = carried(r["EXF"], 0, 1.0)
    chain(start[0], start[1], 1.0, True)
    for k in range(nt_):
        HR[k, 0:8, :] = ST[0, 8 * k : 8 * k + 8, :]
        HI[k, 0:8, :] = ST[1, 8 * k : 8 * k + 8, :]

    def states(n, carry):
        out = []
        for k in range(nt_):
            hr, hi = carry[k]
            c, s = turn8[k]
            lam = LAM[k, rows_of(n), :]
            nr = lam * (c * hr - s * hi) + BR[k, rows_of(n), :]
            ni = lam * (c * hi + s * hr) + BI[k, rows_of(n), :]
            HR[k, rows_of(n + 1), :] = nr
            HI[k, rows_of(n + 1), :] = ni
            out.append((nr, ni))
        return tuple(out)

    lax.fori_loop(
        0,
        steps,
        states,
        tuple((ST[0, 8 * k : 8 * k + 8, :], ST[1, 8 * k : 8 * k + 8, :]) for k in range(nt_)),
        unroll=4,
    )

    half = GROUP // 2
    same = one_hot(cells((LANES, LANES), 0) // half == cells((LANES, LANES), 1) // half)

    def group_mean(v):
        top = v.astype(BF)
        rest = (v - top.astype(F32)).astype(BF)
        return (nn(top, same) + nn(rest, same)) * (1.0 / GROUP)

    NR, NI, RS, MIX = r["NR"], r["NI"], r["RS"], r["MIX"]

    def normalise(k, c):
        hr, hi = HR[k, pl.ds(8, T), :], HI[k, pl.ds(8, T), :]
        mean = group_mean(hr + hi)
        hr, hi = hr - mean, hi - mean
        rstd = lax.rsqrt(group_mean(hr * hr + hi * hi) + 1e-05)
        RS[k] = rstd
        hr, hi = hr * rstd, hi * rstd
        NR[k] = hr
        NI[k] = hi
        gr, gi = ACT[k, :, 384:512], ACT[k, :, 512:640]
        MIX[k, :, 0:128] = (hr * PAR[k, 2:3, :] * (gr * jax.nn.sigmoid(gr))).astype(BF)
        MIX[k, :, 128:256] = (hi * PAR[k, 3:4, :] * (gi * jax.nn.sigmoid(gi))).astype(BF)
        return c

    lax.fori_loop(0, nt_, normalise, 0)

    def slot(k):
        return lax.rem(k + nt_ - z, nt_)

    RES, MID = r["RES"], r["MID"]
    RES[...] = X[...]

    def mix_in(k, c):
        RES[...] += nn(MIX[slot(k)], WXP[slot(k)])
        return c

    lax.fori_loop(0, nt_, mix_in, 0)

    norm_rows(RES, r["g2"], MID)

    HID, DG = r["HID"], r["DG"]

    def gate_w(k, h):
        return WM[h, :, pl.ds(k, 1), 0:96, :].reshape(768, 384)

    def down_w(k, h):
        return WM[h, :, pl.ds(k, 1), 96:144, :].reshape(384, 384)

    def swiglu(k):
        def tile(i, c):
            at = pl.ds(pl.multiple_of(i * 256, 256), 256)
            ga = nn(MID[at, :], gate_w(k, 0))
            ua = nn(MID[at, :], gate_w(k, 1))
            gh = nt(GY[at, 0:384], down_w(k, 0)) + nt(GY[at, 384:768], down_w(k, 1))
            s = jax.nn.sigmoid(ga)
            sl = ga * s
            HID[k, at, :] = (sl * ua).astype(BF)
            DG[k, at, 0:384] = (gh * ua * (s * (1.0 + ga * (1.0 - s)))).astype(BF)
            DG[k, at, 384:768] = (gh * sl).astype(BF)
            return c

        lax.fori_loop(0, T // 256, tile, 0)

    swiglu(0)
    SM = r["SM"]
    for h in range(2):
        SM[h, :, 0:96, :] = tn(MID[...], DG[0, :, 384 * h : 384 * h + 384]).astype(BF).reshape(8, 96, 384)
        SM[h, :, 96:144, :] = (
            tn(HID[0], GY[:, 384 * h : 384 * h + 384]).astype(BF).reshape(8, 48, 384)
        )

    class Summed:
        def __init__(self, parts):
            self.parts = parts
            self.todo = []

        def stage(self, n):
            for copy in self.todo:
                copy.wait_recv()
            self.todo = []
            for bufs in self.parts:
                for h in range(2):
                    f, s = order[h]
                    S = bufs[0]
                    spans = (
                        (0, 0, 4),
                        (f, bits[0] * 4, 2),
                        (s, bits[0] * 4 + bits[f] * 2, 1),
                    )
                    if 1 <= n <= 3:
                        b, start, count = spans[n - 1]
                        mine = pl.ds(start + bits[b] * count, count)
                        S[h, mine] = (S[h, mine].astype(F32) + bufs[n][h].astype(F32)).astype(BF)
                    if n == 3:
                        part = pl.ds(place[h], 1)
                        for b in range(3, nd.bit_length() - 1):
                            land = bufs[4].at[h, pl.ds(b - 3, 1)]
                            one = links.send(S.at[h, part], land, partner(b))
                            one.wait()
                            links.open = [c for c in links.open if c is not one]
                            S[h, part] = (
                                S[h, part].astype(F32) + bufs[4][h, b - 3 : b - 2].astype(F32)
                            ).astype(BF)
                        bufs[5][h, part] = S[h, part]
                    if n < 3:
                        b, start, count = spans[n]
                        away = start + (1 - bits[b]) * count
                        self.todo.append(
                            links.send(S.at[h, pl.ds(away, count)], bufs[n + 1].at[h], partner(b))
                        )
                    elif n < 6:
                        b, start, count = (
                            (s, place[h], 1),
                            (f, bits[0] * 4 + bits[f] * 2, 2),
                            (0, bits[0] * 4, 4),
                        )[n - 3]
                        part = bufs[5].at[h, pl.ds(start, count)]
                        self.todo.append(links.send(part, part, partner(b)))

    mlp_sum = Summed([(SM, r["SM0"], r["SM1"], r["SM2"], r["SME"], r["SMF"])])
    mlp_sum.stage(0)
    for n in range(6, 9):
        gather_round(n)
        swiglu(n - 5)

    GRES = r["GRES"]
    NAT[...] = jnp.zeros((T, 768), F32)

    def back_mid(k, c):
        j = slot(k)
        NAT[...] += nt(DG[j, :, 0:384], gate_w(j, 0)) + nt(DG[j, :, 384:768], gate_w(j, 1))
        return c

    lax.fori_loop(0, nt_, back_mid, 0)
    mlp_sum.stage(1)
    LOWR = r["MID"]

    def back_second(i, total):
        at = pl.ds(pl.multiple_of(i * 128, 128), 128)
        res, gmid = RES[at, :], NAT[at, :]
        q2 = lax.rsqrt(jnp.mean(res * res, -1, keepdims=True) + 1e-06)
        p = gmid * r["g2"][...]
        back = q2 * p - res * (q2 * q2 * q2) * jnp.mean(p * res, -1, keepdims=True)
        gres = GY[at, :].astype(F32) + back
        GRES[at, :] = gres
        LOWR[at, :] = gres.astype(BF)
        return total + jnp.sum((gmid * res * q2).reshape(16, 8, 768), 0)

    EXV = r["EXV"]
    gnorm2 = down_sum(lax.fori_loop(0, T // 128, back_second, jnp.zeros((8, 768), F32)))
    for i in range(6):
        EXV[me, 6 + i : 7 + i, :] = gnorm2[:, 128 * i : 128 * i + 128]
    mlp_sum.stage(2)

    G = DG

    def back_norm(k, want):
        gact = nt(LOWR[...], WXP[k])
        rstd = RS[k]
        parts, sums, dots = [], 0.0, 0.0
        for i, hn in enumerate((NR[k], NI[k])):
            pre = ACT[k, :, 384 + 128 * i : 512 + 128 * i]
            gain = PAR[k, 2 + i : 3 + i, :]
            ga = gact[:, 128 * i : 128 * i + 128]
            s = jax.nn.sigmoid(pre)
            sl = pre * s
            gh = ga * hn
            G[k, :, 384 + 128 * i : 512 + 128 * i] = (
                gh * gain * (s * (1.0 + pre * (1.0 - s)))
            ).astype(BF)
            if want:
                EXV[me, 14 + i : 15 + i, :] = down_sum(gh * sl)
            p = ga * gain * sl
            parts.append((p, hn))
            sums = sums + p
            dots = dots + p * hn
        sums, dots = group_mean(sums), group_mean(dots)
        for buf, (p, hn) in zip((BR, BI), parts):
            buf[k] = rstd * (p - sums - hn * dots)

    back_norm(0, True)
    lax.fori_loop(1, nt_, lambda k, c: (back_norm(k, False), c)[1], 0)
    mlp_sum.stage(3)

    def back_ends(n, carry):
        n = steps - 1 - n
        out = []
        for k in range(nt_):
            ur, ui = carry[k]
            c, s = turn8[k]
            lam = LAM[k, rows_of(n), :]
            er = BR[k, rows_of(n), :] + ur
            ei = BI[k, rows_of(n), :] + ui
            out.append((lam * (c * er + s * ei), lam * (c * ei - s * er)))
        return tuple(out)

    first = lax.fori_loop(0, steps, back_ends, tuple((zero8, zero8) for k in range(nt_)), unroll=4)
    for k in range(nt_):
        CH[1, 8 * k : 8 * k + 8, :] = first[k][0]
        CH[2, 8 * k : 8 * k + 8, :] = first[k][1]
    post(r["EXB"], 1, *chain(zero4, zero4, -1.0, False))
    SX = r["SX"]
    rows, cols = cells((256, 256), 0), cells((256, 256), 1)
    lane = rows % 128
    together = one_hot((cols == 2 * lane + rows // 128) & (lane < ch))
    low_mix = nn(MIX[0], together).astype(BF)
    for h in range(2):
        SX[h] = tn(low_mix, LOWR[:, 384 * h : 384 * h + 384]).astype(BF).reshape(8, 32, 384)
    mlp_sum.stage(4)

    start = carried(r["EXB"], 1, -1.0)
    chain(start[0], start[1], -1.0, True)

    def back_states(n, carry):
        n = steps - 1 - n
        out = []
        for k in range(nt_):
            ur, ui = carry[k]
            c, s = turn8[k]
            lam = LAM[k, rows_of(n), :]
            er = BR[k, rows_of(n), :] + ur
            ei = BI[k, rows_of(n), :] + ui
            BR[k, rows_of(n), :] = er
            BI[k, rows_of(n), :] = ei
            out.append((lam * (c * er + s * ei), lam * (c * ei - s * er)))
        return tuple(out)

    lax.fori_loop(
        0,
        steps,
        back_states,
        tuple((ST[0, 8 * k : 8 * k + 8, :], ST[1, 8 * k : 8 * k + 8, :]) for k in range(nt_)),
        unroll=4,
    )

    def back_gates(k, c, s, want):
        er, ei = BR[k], BI[k]
        hr, hi = HR[k, pl.ds(0, T), :], HI[k, pl.ds(0, T), :]
        gap = PAR[k, 0:1, :]
        gar, gai = er * hr + ei * hi, ei * hr - er * hi
        ur, ui, fg = ACT[k, :, 0:128], ACT[k, :, 128:256], ACT[k, :, 256:384]
        su, si, sf = jax.nn.sigmoid(ur), jax.nn.sigmoid(ui), jax.nn.sigmoid(-fg)
        leak = gap * sf
        gleak = er * (ur * su) + ei * (ui * si) - (c * gar + s * gai)
        G[k, :, 0:128] = (er * leak * (su * (1.0 + ur * (1.0 - su)))).astype(BF)
        G[k, :, 128:256] = (ei * leak * (si * (1.0 + ui * (1.0 - si)))).astype(BF)
        G[k, :, 256:384] = (-gleak * leak * (1.0 - sf)).astype(BF)
        if want:
            EXV[me, 12:13, :] = down_sum(gleak * sf)
            EXV[me, 13:14, :] = down_sum((1.0 - leak) * (c * gai - s * gar))

    back_gates(0, turn[0][0], turn[0][1], True)

    SI = r["SI"]
    rows, cols = cells((640, 512), 0), cells((640, 512), 1)
    lane, g = rows % 128, rows // 128
    to = jnp.where(
        g < 2,
        2 * lane + g,
        jnp.where(g == 2, 2 * ch + lane, 3 * ch + 2 * lane + (g - 3)),
    )
    gcat = nn(G[0, :, 0:640], one_hot((cols == to) & (lane < ch))).astype(BF)
    for h in range(2):
        SI[h] = tn(LOW[:, 384 * h : 384 * h + 384], gcat).astype(BF).reshape(8, 48, 512)
    rec_sum = Summed(
        [(SI, r["SI0"], r["SI1"], r["SI2"], r["SIE"], r["SIF"]), (SX, r["SX0"], r["SX1"], r["SX2"], r["SXE"], r["SXF"])]
    )
    rec_sum.stage(0)
    mlp_sum.stage(5)
    for k in range(1, nt_):
        back_gates(k, turn[k][0], turn[k][1], False)
    rec_sum.stage(1)

    NAT[...] = jnp.zeros((T, 768), F32)

    def back_in(k, c):
        NAT[...] += nn(G[slot(k), :, 0:640], WRP[slot(k)])
        return c

    lax.fori_loop(0, nt_, back_in, 0)
    rec_sum.stage(2)
    def back_first(i, total):
        at = pl.ds(pl.multiple_of(i * 128, 128), 128)
        x, gin = X[at, :], NAT[at, :]
        q1 = lax.rsqrt(jnp.mean(x * x, -1, keepdims=True) + 1e-06)
        p = gin * r["g1"][...]
        GRES[at, :] += q1 * p - x * (q1 * q1 * q1) * jnp.mean(p * x, -1, keepdims=True)
        return total + jnp.sum((gin * x * q1).reshape(16, 8, 768), 0)

    gnorm1 = down_sum(lax.fori_loop(0, T // 128, back_first, jnp.zeros((8, 768), F32)))
    for i in range(6):
        EXV[me, i : i + 1, :] = gnorm1[:, 128 * i : 128 * i + 128]
    exchange(2, EXV, "go")
    rec_sum.stage(3)

    finals = []

    def put_out(src, dst, k):
        copy = pltpu.make_async_copy(src, dst, r["out"].at[k])
        copy.start()
        finals.append(copy)

    def put_from(buf):
        def put(k, c):
            for i in range(6):
                PERM[i, pl.ds(k, 8, stride=steps), :] = buf[pl.ds(pl.multiple_of(8 * k, 8), 8), tiles[i]]
            return c

        lax.fori_loop(0, steps, put, 0, unroll=4)

    put_from(GRES)
    for i in range(6):
        NAT[:, tiles[i]] = PERM[i]
    put_out(NAT, r["tok"], 0)
    rec_sum.stage(4)

    def down(k, c):
        j = slot(k)
        for h in range(2):
            RES[:, 384 * h : 384 * h + 384] += nn(HID[j], down_w(j, h))
        return c

    lax.fori_loop(0, nt_, down, 0)

    put_from(RES)
    for i in range(6):
        r["GRES0"][:, tiles[i]] = PERM[i].astype(BF)
    put_out(r["GRES0"], r["mixed"], 1)
    rec_sum.stage(5)

    exchange(2, EXV, "arrive")
    total = EXV[0]
    for k in range(1, nd):
        total = total + EXV[k]
    r["vec"][...] = total
    mlp_sum.stage(6)
    put_out(r["SMF"], r["o_mlp"], 2)
    rec_sum.stage(6)
    put_out(r["SIF"], r["o_in"], 3)
    put_out(r["SXF"], r["o_mix"], 4)
    for which in range(3):
        exchange(which, (r["EXF"], r["EXB"], EXV)[which], "leave")
    links.drain()
    for copy in finals:
        copy.wait()


def local(nd, nt_, *args):
    (tokens, cot, g1, w_in, w_f, w_o, gap, phase, gg, w_mix, g2, wg, wu, wd) = args
    T, D = tokens.shape
    ch = w_f.shape[1]
    given = dict(
        tokens=tokens,
        cot=cot,
        g1=g1.reshape(1, D),
        w_in=w_in,
        w_f=w_f,
        w_o=w_o,
        gap=gap.reshape(1, ch),
        phase=phase.reshape(1, ch),
        gg=gg.reshape(1, 2 * ch),
        w_mix=w_mix,
        g2=g2.reshape(1, D),
        wg=wg.reshape(8, 96, 384),
        wu=wu.reshape(8, 96, 384),
        wd=wd.reshape(8, 48, D),
    )
    vmem = pl.BlockSpec(memory_space=pltpu.VMEM)
    in_specs = [pl.BlockSpec(memory_space=pl.ANY) if k in ("wg", "wu", "wd", "tokens", "cot") else vmem for k in given]
    outs = dict(
        mixed=jax.ShapeDtypeStruct((T, D), BF),
        tok=jax.ShapeDtypeStruct((T, D), F32),
        o_mlp=jax.ShapeDtypeStruct((2, 8, 144, 384), BF),
        o_in=jax.ShapeDtypeStruct((2, 8, 48, 512), BF),
        o_mix=jax.ShapeDtypeStruct((2, 8, 32, 384), BF),
        vec=jax.ShapeDtypeStruct((16, LANES), F32),
    )
    scratch = scratch_list(nd, nt_, T)
    names = list(given) + list(outs) + list(scratch)
    mixed, tok, o_mlp, o_in, o_mix, vec = pl.pallas_call(
        functools.partial(kernel, nd, nt_, T, names),
        out_shape=list(outs.values()),
        in_specs=in_specs,
        out_specs=[vmem if k == "vec" else pl.BlockSpec(memory_space=pl.ANY) for k in outs],
        scratch_shapes=list(scratch.values()),
        compiler_params=pltpu.CompilerParams(
            collective_id=0, has_side_effects=True, vmem_limit_bytes=63 * 2**20
        ),
    )(*given.values())

    grad_gate = o_mlp[0, :, 0:96].reshape(D, 384).astype(F32)
    grad_up = o_mlp[1, :, 0:96].reshape(D, 384).astype(F32)
    grad_down = (
        o_mlp[:, :, 96:144].reshape(2, 384, 384).transpose(1, 0, 2).reshape(384, D).astype(F32)
    )
    g_in = o_in.reshape(D, 512)
    grad_input = g_in[:, 0 : 2 * ch].astype(F32)
    grad_forget = g_in[:, 2 * ch : 3 * ch].astype(F32)
    grad_outgate = g_in[:, 3 * ch : 5 * ch].astype(F32)
    grad_mix = o_mix.reshape(2, 256, 384)[:, : 2 * ch].transpose(1, 0, 2).reshape(2 * ch, D).astype(F32)
    grad_group = jnp.stack([vec[14, :ch], vec[15, :ch]], -1).reshape(2 * ch)
    return (
        mixed,
        tok,
        vec[0:6].reshape(D),
        grad_input,
        grad_forget,
        grad_outgate,
        vec[12, :ch],
        vec[13, :ch],
        grad_group,
        grad_mix,
        vec[6:12].reshape(D),
        grad_gate,
        grad_up,
        grad_down,
    )


def solution(mesh):
    in_specs = (
        P("dp", None),
        P("dp", None),
        P(),
        P(None, "tp"),
        P(None, "tp"),
        P(None, "tp"),
        P("tp"),
        P("tp"),
        P("tp"),
        P("tp", None),
        P(),
        P(None, "tp"),
        P(None, "tp"),
        P("tp", None),
    )
    out_specs = (
        P("dp", None),
        P("dp", None),
        P(),
        P(None, "tp"),
        P(None, "tp"),
        P(None, "tp"),
        P("tp"),
        P("tp"),
        P("tp"),
        P("tp", None),
        P(),
        P(None, "tp"),
        P(None, "tp"),
        P("tp", None),
    )
    body = functools.partial(local, mesh.shape["dp"], mesh.shape["tp"])
    return jax.shard_map(body, mesh=mesh, in_specs=in_specs, out_specs=out_specs, check_vma=False)
```

time: 652 us -> 139 us (0.21)
  waiting for transfers between devices: 299 us -> 0 us
  local copies, waits for them, and re-layouts: 136 us -> 15.8 us
  Pallas kernels: 0 us -> 117 us
  blocking collectives: 84.8 us -> 0 us
  other arithmetic: 78.9 us -> 4.3 us
  matrix products: 28.9 us -> 0 us
  between operations: 20 us -> 0.77 us
    psum x4 -> x0, waiting for transfers between devices: 299 us -> none  [the longest x1 106 us: local(): lax.psum(product(hidden, w_down), 'tp')]
    pallas_call x0 -> x1, Pallas kernels: none -> 117 us  [local(): pl.pallas_call(functools.partial(kernel, nd, nt_, T, names), out_shape=li...]
    pad x188 -> x0, local copies, waits for them, and re-layouts: 71.1 us -> none  [recurrence(): lax.associative_scan(combine, (retain * jnp.cos(phase_angle), retain * jn...]
    all_gather x5 -> x0, blocking collectives: 47 us -> none  [prefix(): everything = jax.tree.map(lambda part: lax.all_gather(part, axis), shard)]
    add_any x75 -> x0, other arithmetic: 32.2 us -> none  [the longest x18 10.6 us: combine(): latter[0] * earlier[0] - latter[1] * earlier[1]]
    slice x192 -> x4, local copies, waits for them, and re-layouts: 33.8 us -> 2.79 us  [the longest x1 1.36 us: local(): grad_up = o_mlp[1, :, 0:96].reshape(D, 384).astype(F32)]
    dot_general x24 -> x0, matrix products: 28.9 us -> none  [the longest x8 10.9 us: over_rows(): lax.dot_general(left_side, right_side, (((0,), (0,)), ((), ())), preferre...]
    psum x1 -> x0, blocking collectives: 25.1 us -> none  [local(): lax.psum((grad_norm1, grad_input, grad_forget, grad_outgate, grad_gap, gr...]
  transfers between devices with their start and end apart: 4 -> 0, of which waited for: 4 -> 0; matrix products, arithmetic and copies ran while one was open for 4% -> 0% of each run, Pallas kernels for 0% -> 0%
where the time goes in v1:
time: 139 us; the launch traced here: 138 us
  Pallas kernels  117 us (84%)
  local copies, waits for them, and re-layouts  15.8 us (11%)
  other arithmetic  4.3 us (3%)
    pallas_call x1, Pallas kernels, local(): pl.pallas_call(functools.partial(kernel, nd, nt_, T, names), out_shape=li...  117 us
    unnamed x24, local copies, waits for them, and re-layouts  7.13 us

profile of v1, /device:TPU:0, one launch (start us, length us, event | category | flops | bytes accessed | tf_op | source)
XLA Modules:
  0.0 137.7 jit_solution(9676622010246343193)
XLA Ops:
  0.6 0.0 copy-start.4
  0.7 0.0 copy-start.6
  0.7 0.0 copy-start.7
  0.7 1.9 %copy.36.refs_3_ = bf16[768,192]{1,0:T(8,128)(2,1)} copy(bf16[768,192]{0,1:T(8,128)(2,1)} %param.17) | data formatting | bytes 589824 | tf_op args[3]
  2.6 1.9 %copy.38.refs_5_ = bf16[768,192]{1,0:T(8,128)(2,1)} copy(bf16[768,192]{0,1:T(8,128)(2,1)} %param.19) | data formatting | bytes 589824 | tf_op args[5]
  4.5 0.0 copy-done.4
  4.5 0.8 copy.37.refs_4_
  5.3 0.6 reshape.80.refs_2_
  5.9 0.6 reshape.84.refs_10_
  6.5 116.9 %shard_map.245 = (bf16[512,768]{1,0:T(8,128)(2,1)}, f32[512,768]{1,0:T(8,128)}, bf16[2,8,144,384]{3,2,1,0:T(8,128)(2,1)}, bf16[2,8,48,512]{3,2,1,0:T(8,128)(2,1)...) custom-call(bf16[512,768]{1,0:T(8,128)(2,1)} %refs_0_.1, bf16[512,768]{1,0:T(8,128)(2,1)} %refs_1_.1, ...), custom_call_target="tpu_custom_call" | custom-call | tf_op jit(solution)/shard_map/pallas_call | solution.py:870
  123.3 1.3 slice_bitcast_fusion.3
  124.7 0.1 copy.42
  124.8 0.7 reshape.90
  125.5 1.4 fusion
  126.9 0.0 copy-start.1
  126.9 1.7 %bitcast_convert_fusion = (f32[768,384]{1,0:T(8,128)}, f32[768,384]{1,0:T(8,128)}) fusion(bf16[1,8,96,384]{3,2,1,0:T(8,128)(2,1)S(1)} %get-tuple-element.26, bf16[1,8,96,384]{3,2,1,0:T(8,128)(2,1)S(1)} %get-tuple-element.27), kind=kLoop, calls=%fused_computation.1 | loop fusion | flops 589824 | bytes 3538944 | tf_op jit(solution)/shard_map/convert_element_type | solution.py:882
  128.6 0.2 fusion.1
  128.7 0.2 copy.45
  128.9 0.9 convert_element_type.42
  129.8 0.2 copy.47
  129.9 0.9 convert_element_type.44
  130.8 0.6 slice_bitcast_fusion
  131.4 1.1 slice.51
  132.5 0.1 convert_bitcast_fusion
  132.7 1.1 copy.49
  133.8 0.1 slice.53
  133.9 0.1 copy.46
  134.0 0.7 convert_element_type.43
  134.8 0.9 copy.48
  135.7 0.0 copy-done.2
  135.7 0.9 copy.52
  136.6 1.1 copy.53
  (12 shorter events, 0.1 us)
Async XLA Ops:
  0.6 3.9 %copy-start.4 = (bf16[768,96]{0,1:T(8,128)(2,1)S(1)}, bf16[768,96]{0,1:T(8,128)(2,1)}, u32[]{:S(2)}) copy-start(bf16[768,96]{0,1:T(8,128)(2,1)} %param.18) | copy-start | bytes 442372
  0.7 4.7 %copy-start.6 = (f32[768]{0:T(1024)S(1)}, f32[768]{0:T(1024)}, u32[]{:S(2)}) copy-start(f32[768]{0:T(1024)} %param.16) | copy-start | bytes 9220
  0.7 5.2 %copy-start.7 = (f32[768]{0:T(1024)S(1)}, f32[768]{0:T(1024)}, u32[]{:S(2)}) copy-start(f32[768]{0:T(1024)} %param.24) | copy-start | bytes 9220
  126.9 1.7 %copy-start.1 = (bf16[2,8,48,512]{3,2,1,0:T(8,128)(2,1)S(1)}, bf16[2,8,48,512]{3,2,1,0:T(8,128)(2,1)}, u32[]{:S(2)}) copy-start(bf16[2,8,48,512]{3,2,1,0:T(8,128)(2,1)} %get-tuple-element.23) | copy-start | bytes 2359300
  128.9 1.9 %copy-start.5 = (f32[16,128]{1,0:T(8,128)S(1)}, f32[16,128]{1,0:T(8,128)}, u32[]{:S(2)}) copy-start(f32[16,128]{1,0:T(8,128)} %get-tuple-element.22) | copy-start | bytes 24580
  133.8 1.0 copy-start.3
  134.0 1.7 %copy-start.2 = (bf16[512,768]{1,0:T(8,128)(2,1)S(1)}, bf16[512,768]{1,0:T(8,128)(2,1)}, u32[]{:S(2)}) copy-start(bf16[512,768]{1,0:T(8,128)(2,1)} %get-tuple-element.52) | copy-start | bytes 2359300
  134.8 1.8 %copy-start = (f32[512,768]{1,0:T(8,128)S(1)}, f32[512,768]{1,0:T(8,128)}, u32[]{:S(2)}) copy-start(f32[512,768]{1,0:T(8,128)} %get-tuple-element.53) | copy-start | bytes 4718596

commit v2 on v1

v2 whole, which is shorter than its diff:
```python
import functools

import jax
import jax.numpy as jnp
from jax import lax
from jax.experimental import pallas as pl
from jax.experimental.pallas import tpu as pltpu
from jax.sharding import PartitionSpec as P

MESH = pl.DeviceIdType.MESH
BF = jnp.bfloat16
F32 = jnp.float32
GROUP = 64
LANES = 128


def nn(a, b):
    return jnp.dot(a, b, preferred_element_type=F32)


def nt(a, b):
    return lax.dot_general(a, b, (((1,), (1,)), ((), ())), preferred_element_type=F32)


def tn(a, b):
    return lax.dot_general(a, b, (((0,), (0,)), ((), ())), preferred_element_type=F32)


def exact(a, b, dims):
    return lax.dot_general(
        a, b, (dims, ((), ())), precision=lax.Precision.HIGHEST, preferred_element_type=F32
    )


def cells(shape, axis):
    return lax.broadcasted_iota(jnp.int32, shape, axis)


def one_hot(flags):
    return jnp.where(flags, 1.0, 0.0).astype(BF)


def down_sum(v):
    if v.shape[0] > 8:
        v = jnp.sum(v.reshape(v.shape[0] // 8, 8, v.shape[1]), 0)
    v = v[0:4] + v[4:8]
    v = v[0:2] + v[2:4]
    return v[0:1] + v[1:2]


def power(c, s, n):
    out = None
    while n:
        if n % 2:
            out = (c, s) if out is None else (out[0] * c - out[1] * s, out[0] * s + out[1] * c)
        c, s = c * c - s * s, 2.0 * c * s
        n //= 2
    return out


def sum_buffers(name, nd, rows):
    further = max(1, nd.bit_length() - 4)
    counts = (("", 8), ("0", 4), ("1", 2), ("2", 1), ("E", further), ("F", 8))
    return {name + k: pltpu.VMEM((2, n, rows, 384), BF) for k, n in counts}


def scratch_list(nd, nt_, T):
    dma = pltpu.SemaphoreType.DMA
    return dict(
        RI=pltpu.VMEM((192, 768), BF),
        RF=pltpu.VMEM((96, 768), BF),
        RO=pltpu.VMEM((192, 768), BF),
        RM=pltpu.VMEM((192, 768), BF),
        WI=pltpu.VMEM((2, 8, nt_, 64, 384), BF),
        WX=pltpu.VMEM((2, 4, nt_, 48, 384), BF),
        WM=pltpu.VMEM((2, 8, nt_, 144, 384), BF),
        PAR=pltpu.VMEM((nt_, 8, LANES), F32),
        WRP=pltpu.VMEM((nt_, 640, 768), BF),
        WXP=pltpu.VMEM((nt_, 256, 768), BF),
        PERM=pltpu.VMEM((6, T, LANES), F32),
        X=pltpu.VMEM((T, 768), F32),
        GY=pltpu.VMEM((T, 768), BF),
        LOW=pltpu.VMEM((T, 768), BF),
        ACT=pltpu.VMEM((nt_, T, 640), F32),
        LAM=pltpu.VMEM((nt_, T, LANES), F32),
        BR=pltpu.VMEM((nt_, T, LANES), F32),
        BI=pltpu.VMEM((nt_, T, LANES), F32),
        HR=pltpu.VMEM((nt_, T + 8, LANES), F32),
        HI=pltpu.VMEM((nt_, T + 8, LANES), F32),
        NR=pltpu.VMEM((nt_, T, LANES), F32),
        NI=pltpu.VMEM((nt_, T, LANES), F32),
        RS=pltpu.VMEM((nt_, T, LANES), F32),
        MIX=pltpu.VMEM((nt_, T, 256), BF),
        RES=pltpu.VMEM((T, 768), F32),
        MID=pltpu.VMEM((T, 768), BF),
        COT=pltpu.VMEM((T, 768), BF),
        HID=pltpu.VMEM((nt_, T, 384), BF),
        DG=pltpu.VMEM((nt_, T, 768), BF),
        NAT=pltpu.VMEM((T, 768), F32),
        GRES=pltpu.VMEM((T, 768), F32),
        CH=pltpu.VMEM((3, nt_ * 8, LANES), F32),
        ST=pltpu.VMEM((2, nt_ * 8, LANES), F32),
        EX0=pltpu.VMEM((nd, 16, LANES), F32),
        EX1=pltpu.VMEM((nd, 16, LANES), F32),
        EX2=pltpu.VMEM((nd, 16, LANES), F32),
        EX3=pltpu.VMEM((nd, 16, LANES), F32),
        **sum_buffers("SM", nd, 144),
        **sum_buffers("SE", nd, 48),
        **sum_buffers("SL", nd, 48),
        loc=dma((16,)),
        out=dma((8,)),
        ss=dma((160,)),
        rs=dma((160,)),
        es=dma((4, nd)),
        er=dma((4, nd)),
    )


class Links:
    def __init__(self, ss, rs):
        self.ss, self.rs, self.used, self.open = ss, rs, 0, []

    def send(self, src, dst, dev):
        k = self.used
        self.used += 1
        copy = pltpu.make_async_remote_copy(
            src, dst, self.ss.at[k], self.rs.at[k], device_id=dev, device_id_type=MESH
        )
        copy.start()
        self.open.append(copy)
        return copy

    def drain(self):
        for copy in self.open:
            copy.wait_send()
        self.open = []


def kernel(nd, nt_, T, names, *refs):
    r = dict(zip(names, refs))
    me, z = lax.axis_index("dp"), lax.axis_index("tp")
    steps = T // 8
    ch = r["w_f"].shape[0]
    blocks = list(range(nt_))

    def flip(bit):
        return me + bit - 2 * bit * ((me // bit) % 2)

    bits = (me % 2, (me // 2) % 2, (me // 4) % 2)
    order = ((1, 2), (2, 1))
    place = [bits[0] * 4 + bits[f] * 2 + bits[s] for f, s in order]
    wide = [bits[0] * 2 + bits[f] for f, s in order]
    links = Links(r["ss"], r["rs"])
    away = [0, 1, 3, 2] if nt_ == 4 else blocks

    def slot(k):
        o = lax.rem(k + nt_ - z, nt_)
        if nt_ != 4:
            return o
        return jnp.where(o == 2, 3, jnp.where(o == 3, 2, o))

    barrier = pltpu.get_barrier_semaphore()

    def greet_dp(o, c):
        pl.semaphore_signal(barrier, 1, device_id=(lax.rem(me + o, nd), z), device_id_type=MESH)
        return c

    def greet_tp(o, c):
        pl.semaphore_signal(barrier, 1, device_id=(me, lax.rem(z + o, nt_)), device_id_type=MESH)
        return c

    lax.fori_loop(1, nt_, greet_tp, 0)
    lax.fori_loop(1, nd, greet_dp, 0)

    WM = r["WM"]
    loads = {}
    for k, (name, src, dst) in enumerate(
        (
            ("w_i", r["w_i"], r["RI"]),
            ("w_f", r["w_f"], r["RF"]),
            ("w_o", r["w_o"], r["RO"]),
            ("tokens", r["tokens"], r["MID"]),
            ("w_x", r["w_mix"], r["RM"]),
            ("g", r["wg"], WM.at[0, :, 0, 0:96, :]),
            ("u", r["wu"], WM.at[1, :, 0, 0:96, :]),
            ("d0", r["wd"].at[:, :, 0:384], WM.at[0, :, 0, 96:144, :]),
            ("d1", r["wd"].at[:, :, 384:768], WM.at[1, :, 0, 96:144, :]),
            ("cot", r["cot"], r["COT"]),
        )
    ):
        loads[name] = pltpu.make_async_copy(src, dst, r["loc"].at[k])
        loads[name].start()

    WI, WX, WRP, WXP, PAR = r["WI"], r["WX"], r["WRP"], r["WXP"], r["PAR"]
    rows, cols = cells((2 * ch, 2 * ch), 0), cells((2 * ch, 2 * ch), 1)
    apart = one_hot(cols == jnp.where(rows < ch, 2 * rows, 2 * (rows - ch) + 1))
    for k in ("w_i", "w_f", "w_o"):
        loads[k].wait()
    turned = jnp.concatenate(
        [
            nn(apart, r["RI"][...]).astype(BF),
            r["RF"][...],
            nn(apart, r["RO"][...]).astype(BF),
            jnp.zeros((32, 768), BF),
        ],
        axis=0,
    )
    for h in range(2):
        for p in range(8):
            WI[h, p, 0] = turned[64 * p : 64 * p + 64, 384 * h : 384 * h + 384]
    PAR[0] = jnp.zeros((8, LANES), F32)
    PAR[0, 0:1, 0:ch] = r["gap"][...]
    PAR[0, 1:2, 0:ch] = r["phase"][...]
    gains = exact(
        jnp.broadcast_to(r["gg"][...], (8, 2 * ch)), apart.astype(F32), ((1,), (1,))
    )
    PAR[0, 2:3, 0:ch] = gains[0:1, 0:ch]
    PAR[0, 3:4, 0:ch] = gains[0:1, ch : 2 * ch]

    def across(o):
        return (me, lax.rem(z + nt_ - o, nt_))

    def partner(b):
        return (flip(1 << b), z)

    class Unit:
        def __init__(self, buf, slots, portions):
            self.buf, self.slots, self.portions = buf, slots, portions
            self.todo = []

        def wait(self):
            for copy in self.todo:
                copy.wait_recv()
            self.todo = []

        def hop(self, h, b, start, count):
            part = self.buf.at[h, pl.ds(start, count), pl.ds(self.slots[0], len(self.slots))]
            self.todo.append(links.send(part, part, partner(b)))

        def z(self):
            for s in self.slots:
                for h in range(2):
                    at = place[h] if self.portions == 8 else wide[h]
                    self.todo.append(
                        links.send(self.buf.at[h, at, 0], self.buf.at[h, at, s], across(away[s]))
                    )

        def s(self):
            self.wait()
            for h in range(2):
                f, s = order[h]
                if self.portions == 8:
                    self.hop(h, s, place[h], 1)
                else:
                    self.hop(h, f, wide[h], 1)

        def f(self):
            self.wait()
            for h in range(2):
                f, s = order[h]
                self.hop(h, f, bits[0] * 4 + bits[f] * 2, 2)

        def c(self):
            self.wait()
            n = self.portions // 2
            for h in range(2):
                self.hop(h, 0, bits[0] * n, n)

    I1, I2 = Unit(WI, blocks[1:3], 8), Unit(WI, blocks[3:], 8)
    XM = Unit(WX, blocks[1:], 4)
    M1, M2, M3 = [Unit(WM, [s], 8) for s in blocks[1:]]

    pl.semaphore_wait(barrier, nd - 1 + nt_ - 1)
    I1.z()
    par_copies = [links.send(PAR.at[0], PAR.at[s], across(away[s])) for s in blocks[1:]]

    PERM, X, GY, LOW = r["PERM"], r["X"], r["GY"], r["LOW"]
    loads["tokens"].wait()
    tiles = [slice(LANES * i, LANES * i + LANES) for i in range(6)]
    for i in range(6):
        PERM[i] = r["MID"][:, tiles[i]].astype(F32)

    def take(k, c):
        for i in range(6):
            X[pl.ds(pl.multiple_of(8 * k, 8), 8), tiles[i]] = PERM[i, pl.ds(k, 8, stride=steps), :]
        return c

    lax.fori_loop(0, steps, take, 0, unroll=4)

    def whole_row(ref):
        return jnp.concatenate([ref[i : i + 1, :] for i in range(6)], axis=1)

    gain1, gain2 = whole_row(r["g1"]), whole_row(r["g2"])

    def norm_rows(src, gain, dst):
        def body(i, c):
            at = pl.ds(pl.multiple_of(i * 128, 128), 128)
            v = src[at, :]
            q = lax.rsqrt(jnp.mean(v * v, -1, keepdims=True) + 1e-06)
            dst[at, :] = (v * q * gain).astype(BF)
            return c

        lax.fori_loop(0, T // 128, body, 0)

    norm_rows(X, gain1, LOW)
    I2.z()

    for k in blocks:
        for g in range(5):
            WRP[k, g * 128 + 96 : g * 128 + 128, :] = jnp.zeros((32, 768), BF)
        for g in range(2):
            WXP[k, g * 128 + 96 : g * 128 + 128, :] = jnp.zeros((32, 768), BF)

    def spread_in(k):
        for g in range(5):
            for q in range(3):
                row = g * 96 + q * 32
                for h in range(2):
                    WRP[k, g * 128 + q * 32 : g * 128 + q * 32 + 32, 384 * h : 384 * h + 384] = WI[
                        h, row // 64, k, row % 64 : row % 64 + 32, :
                    ]

    def spread_mix(k):
        for p in range(4):
            row = (p // 2) * 128 + (p % 2) * 48
            for h in range(2):
                WXP[k, row : row + 48, 384 * h : 384 * h + 384] = WX[h, p, k]

    ACT, LAM, BR, BI = r["ACT"], r["LAM"], r["BR"], r["BI"]

    def project(k):
        spread_in(k)
        gap = PAR[k, 0:1, :]
        ACT[k] = nt(LOW[...], WRP[k])
        ur, ui, fg = ACT[k, :, 0:128], ACT[k, :, 128:256], ACT[k, :, 256:384]
        leak = gap * jax.nn.sigmoid(-fg)
        LAM[k] = 1.0 - leak
        BR[k] = leak * (ur * jax.nn.sigmoid(ur))
        BI[k] = leak * (ui * jax.nn.sigmoid(ui))

    loads["w_x"].wait()
    mixed_rows = nn(apart, r["RM"][...]).astype(BF)
    for h in range(2):
        for p in range(4):
            WX[h, p, 0] = mixed_rows[48 * p : 48 * p + 48, 384 * h : 384 * h + 384]
    spread_mix(0)
    I1.s()
    XM.z()
    project(0)
    for k in ("g", "u", "d0", "d1", "cot"):
        loads[k].wait()
    I1.f()
    I2.s()
    M1.z()

    for i in range(6):
        PERM[i] = r["COT"][:, tiles[i]].astype(F32)

    def take_cot(k, c):
        for i in range(6):
            two = [PERM[i, pl.ds(2 * k + j, 8, stride=steps), :] for j in range(2)]
            GY[pl.ds(pl.multiple_of(16 * k, 16), 16), tiles[i]] = jnp.concatenate(two, axis=0).astype(BF)
        return c

    lax.fori_loop(0, steps // 2, take_cot, 0, unroll=2)
    I2.f()
    I1.c()
    XM.s()
    M2.z()
    for copy in par_copies:
        copy.wait_recv()
    I1.wait()
    lax.fori_loop(1, 3, lambda k, c: (project(k), c)[1], 0)
    I2.c()
    M1.s()
    M3.z()
    XM.c()
    I2.wait()
    project(3)
    M1.f()

    CH, ST, HR, HI = r["CH"], r["ST"], r["HR"], r["HI"]
    turn = []
    for k in blocks:
        ph = PAR[k, 1:2, :]
        turn.append((jnp.cos(ph), jnp.sin(ph)))
    turn8 = [(jnp.broadcast_to(c, (8, LANES)), jnp.broadcast_to(s, (8, LANES))) for c, s in turn]
    cos4 = jnp.concatenate([c for c, s in turn], axis=0)
    sin4 = jnp.concatenate([s for c, s in turn], axis=0)
    chunk_c, chunk_s = power(cos4, sin4, steps)
    whole_c, whole_s = power(cos4, sin4, T)
    zero8 = jnp.zeros((8, LANES), F32)
    zero4 = jnp.zeros((nt_, LANES), F32)

    def rows_of(k):
        return pl.ds(pl.multiple_of(8 * k, 8), 8)

    def ends(n, carry):
        out = []
        for k in blocks:
            hr, hi, lp = carry[k]
            c, s = turn8[k]
            lam = LAM[k, rows_of(n), :]
            nr = lam * (c * hr - s * hi) + BR[k, rows_of(n), :]
            ni = lam * (c * hi + s * hr) + BI[k, rows_of(n), :]
            out.append((nr, ni, lp * lam))
        return tuple(out)

    last = lax.fori_loop(0, steps, ends, tuple((zero8, zero8, zero8 + 1.0) for k in blocks), unroll=4)
    for k in blocks:
        CH[0, 8 * k : 8 * k + 8, :] = last[k][2]
        CH[1, 8 * k : 8 * k + 8, :] = last[k][0]
        CH[2, 8 * k : 8 * k + 8, :] = last[k][1]

    def chunk(i, c):
        return CH[i, pl.ds(c, nt_, stride=8), :]

    def chain(sr, si, sign, keep):
        for c in range(8) if sign > 0 else range(7, -1, -1):
            if keep:
                ST[0, pl.ds(c, nt_, stride=8), :] = sr
                ST[1, pl.ds(c, nt_, stride=8), :] = si
            lp = chunk(0, c)
            pr, pi = lp * chunk_c, sign * (lp * chunk_s)
            sr, si = pr * sr - pi * si + chunk(1, c), pr * si + pi * sr + chunk(2, c)
        return sr, si

    whole_lam = chunk(0, 0)
    for c in range(1, 8):
        whole_lam = whole_lam * chunk(0, c)

    def exchange(which, buf, start):
        def copy_of(o, back):
            at = lax.rem(me + nd - o, nd) if back else lax.rem(me + o, nd)
            row = at if back else me
            return pltpu.make_async_remote_copy(
                buf.at[row],
                buf.at[row],
                r["es"].at[which, o],
                r["er"].at[which, o],
                device_id=(at, z),
                device_id_type=MESH,
            )

        def go(o, c):
            copy_of(o, False).start()
            return c

        def arrive(o, c):
            copy_of(o, True).wait_recv()
            return c

        def leave(o, c):
            copy_of(o, False).wait_send()
            return c

        lax.fori_loop(1, nd, {"go": go, "arrive": arrive, "leave": leave}[start], 0)

    def post(buf, which, sr, si):
        buf[me, 0:4, :] = whole_lam
        buf[me, 4:8, :] = sr
        buf[me, 8:12, :] = si
        buf[me, 12:16, :] = zero4
        exchange(which, buf, "go")

    def carried(buf, which, sign):
        exchange(which, buf, "arrive")

        def lap(k, s):
            at = k if sign > 0 else nd - 1 - k
            reached = (at < me) if sign > 0 else (at > me)
            lp = buf[at, 0:4, :]
            pr, pi = lp * whole_c, sign * (lp * whole_s)
            nr = pr * s[0] - pi * s[1] + buf[at, 4:8, :]
            ni = pr * s[1] + pi * s[0] + buf[at, 8:12, :]
            return jnp.where(reached, nr, s[0]), jnp.where(reached, ni, s[1])

        return lax.fori_loop(0, nd, lap, (zero4, zero4))

    post(r["EX0"], 0, *chain(zero4, zero4, 1.0, False))
    XM.wait()
    lax.fori_loop(1, nt_, lambda k, c: (spread_mix(k), c)[1], 0)
    M2.s()
    start = carried(r["EX0"], 0, 1.0)
    chain(start[0], start[1], 1.0, True)
    for k in blocks:
        HR[k, 0:8, :] = ST[0, 8 * k : 8 * k + 8, :]
        HI[k, 0:8, :] = ST[1, 8 * k : 8 * k + 8, :]

    def states(n, carry):
        out = []
        for k in blocks:
            hr, hi = carry[k]
            c, s = turn8[k]
            lam = LAM[k, rows_of(n), :]
            nr = lam * (c * hr - s * hi) + BR[k, rows_of(n), :]
            ni = lam * (c * hi + s * hr) + BI[k, rows_of(n), :]
            HR[k, rows_of(n + 1), :] = nr
            HI[k, rows_of(n + 1), :] = ni
            out.append((nr, ni))
        return tuple(out)

    def held(k):
        return ST[0, 8 * k : 8 * k + 8, :], ST[1, 8 * k : 8 * k + 8, :]

    lax.fori_loop(0, steps, states, tuple(held(k) for k in blocks), unroll=4)
    M1.c()
    M2.f()

    half = GROUP // 2
    same = one_hot(cells((LANES, LANES), 0) // half == cells((LANES, LANES), 1) // half)

    def group_mean(v):
        top = v.astype(BF)
        rest = (v - top.astype(F32)).astype(BF)
        return (nn(top, same) + nn(rest, same)) * (1.0 / GROUP)

    NR, NI, RS, MIX = r["NR"], r["NI"], r["RS"], r["MIX"]

    def normalise(k, c):
        hr, hi = HR[k, pl.ds(8, T), :], HI[k, pl.ds(8, T), :]
        mean = group_mean(hr + hi)
        hr, hi = hr - mean, hi - mean
        rstd = lax.rsqrt(group_mean(hr * hr + hi * hi) + 1e-05)
        RS[k] = rstd
        hr, hi = hr * rstd, hi * rstd
        NR[k] = hr
        NI[k] = hi
        gr, gi = ACT[k, :, 384:512], ACT[k, :, 512:640]
        MIX[k, :, 0:128] = (hr * PAR[k, 2:3, :] * (gr * jax.nn.sigmoid(gr))).astype(BF)
        MIX[k, :, 128:256] = (hi * PAR[k, 3:4, :] * (gi * jax.nn.sigmoid(gi))).astype(BF)
        return c

    lax.fori_loop(0, nt_, normalise, 0)
    M3.s()

    RES, MID = r["RES"], r["MID"]
    RES[...] = X[...]

    def mix_in(k, c):
        RES[...] += nn(MIX[slot(k)], WXP[slot(k)])
        return c

    lax.fori_loop(0, nt_, mix_in, 0)
    norm_rows(RES, gain2, MID)
    M2.c()
    M3.f()

    HID, DG = r["HID"], r["DG"]

    def gate_w(k, h):
        return WM[h, :, pl.ds(k, 1), 0:96, :].reshape(768, 384)

    def down_w(k, h):
        return WM[h, :, pl.ds(k, 1), 96:144, :].reshape(384, 384)

    def swiglu(k):
        def tile(i, c):
            at = pl.ds(pl.multiple_of(i * 256, 256), 256)
            ga = nn(MID[at, :], gate_w(k, 0))
            ua = nn(MID[at, :], gate_w(k, 1))
            gh = nt(GY[at, 0:384], down_w(k, 0)) + nt(GY[at, 384:768], down_w(k, 1))
            s = jax.nn.sigmoid(ga)
            sl = ga * s
            HID[k, at, :] = (sl * ua).astype(BF)
            DG[k, at, 0:384] = (gh * ua * (s * (1.0 + ga * (1.0 - s)))).astype(BF)
            DG[k, at, 384:768] = (gh * sl).astype(BF)
            return c

        lax.fori_loop(0, T // 256, tile, 0)

    swiglu(0)
    SM = r["SM"]
    for h in range(2):
        SM[h, :, 0:96, :] = (
            tn(MID[...], DG[0, :, 384 * h : 384 * h + 384]).astype(BF).reshape(8, 96, 384)
        )
        SM[h, :, 96:144, :] = (
            tn(HID[0], GY[:, 384 * h : 384 * h + 384]).astype(BF).reshape(8, 48, 384)
        )

    class Summed:
        def __init__(self, name):
            self.bufs = [r[name + k] for k in ("", "0", "1", "2")]
            self.further, self.whole = r[name + "E"], r[name + "F"]
            self.todo = []

        def stage(self, n):
            for copy in self.todo:
                copy.wait_recv()
            self.todo = []
            S = self.bufs[0]
            for h in range(2):
                f, s = order[h]
                spans = ((0, 0, 4), (f, bits[0] * 4, 2), (s, bits[0] * 4 + bits[f] * 2, 1))
                if 1 <= n <= 3:
                    b, first, count = spans[n - 1]
                    mine = pl.ds(first + bits[b] * count, count)
                    S[h, mine] = (S[h, mine].astype(F32) + self.bufs[n][h].astype(F32)).astype(BF)
                if n == 3:
                    part = pl.ds(place[h], 1)
                    for b in range(3, nd.bit_length() - 1):
                        land = self.further.at[h, pl.ds(b - 3, 1)]
                        one = links.send(S.at[h, part], land, partner(b))
                        one.wait()
                        links.open = [c for c in links.open if c is not one]
                        S[h, part] = (
                            S[h, part].astype(F32) + self.further[h, b - 3 : b - 2].astype(F32)
                        ).astype(BF)
                    self.whole[h, part] = S[h, part]
                if n < 3:
                    b, first, count = spans[n]
                    give = first + (1 - bits[b]) * count
                    self.todo.append(
                        links.send(S.at[h, pl.ds(give, count)], self.bufs[n + 1].at[h], partner(b))
                    )
                elif n < 6:
                    b, first, count = (
                        (s, place[h], 1),
                        (f, bits[0] * 4 + bits[f] * 2, 2),
                        (0, bits[0] * 4, 4),
                    )[n - 3]
                    part = self.whole.at[h, pl.ds(first, count)]
                    self.todo.append(links.send(part, part, partner(b)))

    finals = []

    def put_out(src, dst):
        copy = pltpu.make_async_copy(src, dst, r["out"].at[len(finals)])
        copy.start()
        finals.append(copy)

    mlp_sum, early_sum, late_sum = Summed("SM"), Summed("SE"), Summed("SL")
    mlp_sum.stage(0)
    M1.wait()
    swiglu(1)
    M3.c()
    mlp_sum.stage(1)
    M2.wait()
    swiglu(2)
    M3.wait()
    swiglu(3)

    GRES, NAT = r["GRES"], r["NAT"]
    NAT[...] = jnp.zeros((T, 768), F32)

    def back_mid(k, c):
        j = slot(k)
        NAT[...] += nt(DG[j, :, 0:384], gate_w(j, 0)) + nt(DG[j, :, 384:768], gate_w(j, 1))
        return c

    lax.fori_loop(0, nt_, back_mid, 0)
    mlp_sum.stage(2)
    LOWR = r["MID"]

    def back_second(i, total):
        at = pl.ds(pl.multiple_of(i * 128, 128), 128)
        res, gmid = RES[at, :], NAT[at, :]
        q2 = lax.rsqrt(jnp.mean(res * res, -1, keepdims=True) + 1e-06)
        p = gmid * gain2
        back = q2 * p - res * (q2 * q2 * q2) * jnp.mean(p * res, -1, keepdims=True)
        gres = GY[at, :].astype(F32) + back
        GRES[at, :] = gres
        LOWR[at, :] = gres.astype(BF)
        return total + jnp.sum((gmid * res * q2).reshape(16, 8, 768), 0)

    VEC = r["EX3"]
    gnorm2 = down_sum(lax.fori_loop(0, T // 128, back_second, jnp.zeros((8, 768), F32)))
    for i in range(6):
        VEC[me, 6 + i : 7 + i, :] = gnorm2[:, 128 * i : 128 * i + 128]

    G = DG
    rows, cols = cells((256, 256), 0), cells((256, 256), 1)
    lane = rows % 128
    together = one_hot((cols == 2 * lane + rows // 128) & (lane < ch))

    def back_norm(k, own):
        gact = nt(LOWR[...], WXP[k])
        rstd = RS[k]
        parts, sums, dots = [], 0.0, 0.0
        group = []
        for i, hn in enumerate((NR[k], NI[k])):
            pre = ACT[k, :, 384 + 128 * i : 512 + 128 * i]
            gain = PAR[k, 2 + i : 3 + i, :]
            ga = gact[:, 128 * i : 128 * i + 128]
            s = jax.nn.sigmoid(pre)
            sl = pre * s
            gh = ga * hn
            G[k, :, 384 + 128 * i : 512 + 128 * i] = (
                gh * gain * (s * (1.0 + pre * (1.0 - s)))
            ).astype(BF)
            if own:
                group.append(down_sum(gh * sl))
            p = ga * gain * sl
            parts.append((p, hn))
            sums = sums + p
            dots = dots + p * hn
        sums, dots = group_mean(sums), group_mean(dots)
        for buf, (p, hn) in zip((BR, BI), parts):
            buf[k] = rstd * (p - sums - hn * dots)
        if own:
            both = jnp.broadcast_to(jnp.concatenate(group, axis=1), (8, 256))
            both = exact(both, together.astype(F32), ((1,), (0,)))
            VEC[me, 14:15, :] = both[0:1, 0:128]
            VEC[me, 15:16, :] = both[0:1, 128:256]

    def back_step(n, carry, some, keep):
        n = steps - 1 - n
        out = []
        for k, (ur, ui) in zip(some, carry):
            c, s = turn8[k]
            lam = LAM[k, rows_of(n), :]
            er = BR[k, rows_of(n), :] + ur
            ei = BI[k, rows_of(n), :] + ui
            if keep:
                BR[k, rows_of(n), :] = er
                BI[k, rows_of(n), :] = ei
            out.append((lam * (c * er + s * ei), lam * (c * ei - s * er)))
        return tuple(out)

    def back_ends(some, buf, which):
        body = functools.partial(back_step, some=some, keep=False)
        first = lax.fori_loop(0, steps, body, tuple((zero8, zero8) for k in some), unroll=4)
        for k, (ur, ui) in zip(some, first):
            CH[1, 8 * k : 8 * k + 8, :] = ur
            CH[2, 8 * k : 8 * k + 8, :] = ui
        post(buf, which, *chain(zero4, zero4, -1.0, False))

    def back_states(some, buf, which):
        sr, si = carried(buf, which, -1.0)
        chain(sr, si, -1.0, True)
        body = functools.partial(back_step, some=some, keep=True)
        lax.fori_loop(0, steps, body, tuple(held(k) for k in some), unroll=4)

    def back_gates(k, own):
        c, s = turn[k]
        er, ei = BR[k], BI[k]
        hr, hi = HR[k, pl.ds(0, T), :], HI[k, pl.ds(0, T), :]
        gap = PAR[k, 0:1, :]
        gar, gai = er * hr + ei * hi, ei * hr - er * hi
        ur, ui, fg = ACT[k, :, 0:128], ACT[k, :, 128:256], ACT[k, :, 256:384]
        su, si, sf = jax.nn.sigmoid(ur), jax.nn.sigmoid(ui), jax.nn.sigmoid(-fg)
        leak = gap * sf
        gleak = er * (ur * su) + ei * (ui * si) - (c * gar + s * gai)
        G[k, :, 0:128] = (er * leak * (su * (1.0 + ur * (1.0 - su)))).astype(BF)
        G[k, :, 128:256] = (ei * leak * (si * (1.0 + ui * (1.0 - si)))).astype(BF)
        G[k, :, 256:384] = (-gleak * leak * (1.0 - sf)).astype(BF)
        if own:
            VEC[me, 12:13, :] = down_sum(gleak * sf)
            VEC[me, 13:14, :] = down_sum((1.0 - leak) * (c * gai - s * gar))

    back_norm(0, True)
    back_ends([0], r["EX1"], 1)
    mlp_sum.stage(3)

    SE, SL = r["SE"], r["SL"]
    gate_cols = nn(G[0, :, 384:640], together)[:, 0 : 2 * ch].astype(BF)
    mix_cols = nn(MIX[0], together)[:, 0 : 2 * ch].astype(BF)
    for h in range(2):
        at = slice(384 * h, 384 * h + 384)
        SE[h, 0:4] = tn(gate_cols, LOW[:, at]).astype(BF).reshape(4, 48, 384)
        SE[h, 4:8] = tn(mix_cols, LOWR[:, at]).astype(BF).reshape(4, 48, 384)
    early_sum.stage(0)
    lax.fori_loop(1, nt_, lambda k, c: (back_norm(k, False), c)[1], 0)
    mlp_sum.stage(4)
    early_sum.stage(1)
    back_states([0], r["EX1"], 1)
    back_gates(0, True)
    rows, cols = cells((384, 384), 0), cells((384, 384), 1)
    lane, g = rows % 128, rows // 128
    to = jnp.where(g < 2, 2 * lane + g, 2 * ch + lane)
    late_cols = nn(G[0, :, 0:384], one_hot((cols == to) & (lane < ch))).astype(BF)
    for h in range(2):
        SL[h] = tn(late_cols, LOW[:, 384 * h : 384 * h + 384]).astype(BF).reshape(8, 48, 384)
    late_sum.stage(0)
    early_sum.stage(2)

    back_ends(blocks[1:], r["EX2"], 2)
    late_sum.stage(1)
    mlp_sum.stage(5)
    early_sum.stage(3)

    def down(k, c):
        j = slot(k)
        for h in range(2):
            RES[:, 384 * h : 384 * h + 384] += nn(HID[j], down_w(j, h))
        return c

    lax.fori_loop(0, nt_, down, 0)
    late_sum.stage(2)
    early_sum.stage(4)
    back_states(blocks[1:], r["EX2"], 2)
    late_sum.stage(3)
    for k in blocks[1:]:
        back_gates(k, False)
    early_sum.stage(5)
    late_sum.stage(4)
    mlp_sum.stage(6)
    put_out(r["SMF"], r["o_mlp"])

    NAT[...] = jnp.zeros((T, 768), F32)

    def back_in(k, c):
        NAT[...] += nn(G[slot(k), :, 0:640], WRP[slot(k)])
        return c

    lax.fori_loop(0, nt_, back_in, 0)

    def back_first(i, total):
        at = pl.ds(pl.multiple_of(i * 128, 128), 128)
        x, gin = X[at, :], NAT[at, :]
        q1 = lax.rsqrt(jnp.mean(x * x, -1, keepdims=True) + 1e-06)
        p = gin * gain1
        GRES[at, :] += q1 * p - x * (q1 * q1 * q1) * jnp.mean(p * x, -1, keepdims=True)
        return total + jnp.sum((gin * x * q1).reshape(16, 8, 768), 0)

    gnorm1 = down_sum(lax.fori_loop(0, T // 128, back_first, jnp.zeros((8, 768), F32)))
    for i in range(6):
        VEC[me, i : i + 1, :] = gnorm1[:, 128 * i : 128 * i + 128]
    exchange(3, VEC, "go")
    late_sum.stage(5)
    early_sum.stage(6)
    put_out(r["SEF"], r["o_early"])

    def put_from(buf):
        def put(k, c):
            for i in range(6):
                PERM[i, pl.ds(k, 8, stride=steps), :] = buf[pl.ds(pl.multiple_of(8 * k, 8), 8), tiles[i]]
            return c

        lax.fori_loop(0, steps, put, 0, unroll=4)

    put_from(GRES)
    for i in range(6):
        NAT[:, tiles[i]] = PERM[i]
    put_out(NAT, r["tok"])
    put_from(RES)
    for i in range(6):
        r["COT"][:, tiles[i]] = PERM[i].astype(BF)
    put_out(r["COT"], r["mixed"])
    late_sum.stage(6)
    put_out(r["SLF"], r["o_late"])

    exchange(3, VEC, "arrive")
    total = VEC[0]
    for k in range(1, nd):
        total = total + VEC[k]
    r["vec"][...] = total
    for which in range(4):
        exchange(which, r["EX%d" % which], "leave")
    links.drain()
    for copy in finals:
        copy.wait()


def writer(names, *refs):
    r = dict(zip(names, refs))
    sem = r["sem"]
    count = [0]

    def copy(src, dst):
        c = pltpu.make_async_copy(src, dst, sem.at[count[0]])
        count[0] += 1
        c.start()
        return c

    ins = {
        "late": copy(r["late"], r["L"]),
        "early": copy(r["early"], r["E"]),
        "mlp": copy(r["mlp"], r["M"]),
    }
    outs = [copy(r["mixed_in"], r["mixed"]), copy(r["tok_in"], r["tok"])]
    ch = r["gap"].shape[1]
    vec = r["vec"]
    r["gn1"][...] = vec[0:6, :]
    r["gn2"][...] = vec[6:12, :]
    r["gap"][...] = vec[12:13, 0:ch]
    r["phase"][...] = vec[13:14, 0:ch]
    r["group"][...] = jnp.concatenate([vec[14:15, :], vec[15:16, 0 : 2 * ch - LANES]], axis=1)
    for name, a, outs_of in (
        ("late", "L", (("LF", 0, 6, (("g_in", 0, 4), ("g_f", 4, 6))),)),
        ("early", "E", (("EF", 0, 8, (("g_o", 0, 4), ("g_x", 4, 8))),)),
    ):
        ins[name].wait()
        for f, lo, hi, dests in outs_of:
            for h in range(2):
                r[f][lo:hi, :, 384 * h : 384 * h + 384] = r[a][h, lo:hi].astype(F32)
            for dst, p, q in dests:
                outs.append(copy(r[f].at[p:q], r[dst]))
    ins["mlp"].wait()
    for h, name in ((0, "g_g"), (1, "g_u")):
        r["GF"][h] = r["M"][h, :, 0:96, :].astype(F32)
        outs.append(copy(r["GF"].at[h], r[name]))
        r["DF"][:, :, 384 * h : 384 * h + 384] = r["M"][h, :, 96:144, :].astype(F32)
    outs.append(copy(r["DF"], r["g_d"]))
    for c in outs:
        c.wait()


def local(nd, nt_, *args):
    (tokens, cot, g1, w_in, w_f, w_o, gap, phase, gg, w_mix, g2, wg, wu, wd) = args
    T, D = tokens.shape
    ch = w_f.shape[1]
    vmem = pl.BlockSpec(memory_space=pltpu.VMEM)
    hbm = pl.BlockSpec(memory_space=pl.ANY)
    given = dict(
        tokens=tokens,
        cot=cot,
        g1=g1.reshape(6, LANES),
        w_i=w_in.T,
        w_f=w_f.T,
        w_o=w_o.T,
        gap=gap.reshape(1, ch),
        phase=phase.reshape(1, ch),
        gg=gg.reshape(1, 2 * ch),
        w_mix=w_mix,
        g2=g2.reshape(6, LANES),
        wg=wg.reshape(8, 96, 384),
        wu=wu.reshape(8, 96, 384),
        wd=wd.reshape(8, 48, D),
    )
    small = ("g1", "g2", "gap", "phase", "gg", "vec")
    shape = jax.ShapeDtypeStruct
    raw = dict(
        mixed=shape((T, D), BF),
        tok=shape((T, D), F32),
        o_mlp=shape((2, 8, 144, 384), BF),
        o_early=shape((2, 8, 48, 384), BF),
        o_late=shape((2, 8, 48, 384), BF),
        vec=shape((16, LANES), F32),
    )
    scratch = scratch_list(nd, nt_, T)
    mixed, tok, o_mlp, o_early, o_late, vec = pl.pallas_call(
        functools.partial(kernel, nd, nt_, T, list(given) + list(raw) + list(scratch)),
        out_shape=list(raw.values()),
        in_specs=[vmem if k in small else hbm for k in given],
        out_specs=[vmem if k in small else hbm for k in raw],
        scratch_shapes=list(scratch.values()),
        compiler_params=pltpu.CompilerParams(
            collective_id=0, has_side_effects=True, vmem_limit_bytes=63 * 2**20
        ),
        name="layer",
    )(*given.values())

    got = dict(mixed_in=mixed, tok_in=tok, mlp=o_mlp, early=o_early, late=o_late, vec=vec)
    final = dict(
        mixed=shape((T, D), BF),
        tok=shape((T, D), F32),
        gn1=shape((6, LANES), F32),
        g_in=shape((4, 48, D), F32),
        g_f=shape((2, 48, D), F32),
        g_o=shape((4, 48, D), F32),
        gap=shape((1, ch), F32),
        phase=shape((1, ch), F32),
        group=shape((1, 2 * ch), F32),
        g_x=shape((4, 48, D), F32),
        gn2=shape((6, LANES), F32),
        g_g=shape((8, 96, 384), F32),
        g_u=shape((8, 96, 384), F32),
        g_d=shape((8, 48, D), F32),
    )
    held = dict(
        L=pltpu.VMEM((2, 8, 48, 384), BF),
        E=pltpu.VMEM((2, 8, 48, 384), BF),
        M=pltpu.VMEM((2, 8, 144, 384), BF),
        LF=pltpu.VMEM((6, 48, D), F32),
        EF=pltpu.VMEM((8, 48, D), F32),
        GF=pltpu.VMEM((2, 8, 96, 384), F32),
        DF=pltpu.VMEM((8, 48, D), F32),
        sem=pltpu.SemaphoreType.DMA((16,)),
    )
    blocky = ("gn1", "gn2", "gap", "phase", "group")
    outs = pl.pallas_call(
        functools.partial(writer, list(got) + list(final) + list(held)),
        out_shape=list(final.values()),
        in_specs=[vmem if k == "vec" else hbm for k in got],
        out_specs=[vmem if k in blocky else hbm for k in final],
        scratch_shapes=list(held.values()),
        compiler_params=pltpu.CompilerParams(vmem_limit_bytes=32 * 2**20),
        name="writer",
    )(*got.values())
    o = dict(zip(final, outs))
    return (
        o["mixed"],
        o["tok"],
        o["gn1"].reshape(D),
        o["g_in"].reshape(2 * ch, D).T,
        o["g_f"].reshape(ch, D).T,
        o["g_o"].reshape(2 * ch, D).T,
        o["gap"].reshape(ch),
        o["phase"].reshape(ch),
        o["group"].reshape(2 * ch),
        o["g_x"].reshape(2 * ch, D),
        o["gn2"].reshape(D),
        o["g_g"].reshape(D, 384),
        o["g_u"].reshape(D, 384),
        o["g_d"].reshape(384, D),
    )


def solution(mesh):
    in_specs = (
        P("dp", None),
        P("dp", None),
        P(),
        P(None, "tp"),
        P(None, "tp"),
        P(None, "tp"),
        P("tp"),
        P("tp"),
        P("tp"),
        P("tp", None),
        P(),
        P(None, "tp"),
        P(None, "tp"),
        P("tp", None),
    )
    out_specs = (
        P("dp", None),
        P("dp", None),
        P(),
        P(None, "tp"),
        P(None, "tp"),
        P(None, "tp"),
        P("tp"),
        P("tp"),
        P("tp"),
        P("tp", None),
        P(),
        P(None, "tp"),
        P(None, "tp"),
        P("tp", None),
    )
    body = functools.partial(local, mesh.shape["dp"], mesh.shape["tp"])
    return jax.shard_map(body, mesh=mesh, in_specs=in_specs, out_specs=out_specs, check_vma=False)
```

time: 139 us -> 119 us (0.86)
  local copies, waits for them, and re-layouts: 15.8 us -> 6.83 us
  Pallas kernels: 117 us -> 111 us
  other arithmetic: 4.3 us -> 0 us
    pallas_call x1 -> x2, Pallas kernels: 117 us -> 111 us  [the longest x1 107 us: local(): pl.pallas_call(functools.partial(kernel, nd, nt_, T, list(given) + list(r...]
    convert_element_type x4 -> x0, other arithmetic: 4.12 us -> none  [the longest x1 1.67 us: local(): grad_up = o_mlp[1, :, 0:96].reshape(D, 384).astype(F32)]
    slice x4 -> x0, local copies, waits for them, and re-layouts: 2.79 us -> none  [the longest x1 1.36 us: local(): grad_up = o_mlp[1, :, 0:96].reshape(D, 384).astype(F32)]
    reshape x4 -> x0, local copies, waits for them, and re-layouts: 2.46 us -> none  [the longest x1 0.7 us: local(): grad_group = jnp.stack([vec[14, :ch], vec[15, :ch]], -1).reshape(2 * ch)]
    convert_element_type x2 -> x0, local copies, waits for them, and re-layouts: 1.96 us -> none  [the longest x1 1.1 us: local(): o_mlp[:, :, 96:144].reshape(2, 384, 384).transpose(1, 0, 2).reshape(384, D)]
    another operation x2 -> x0, local copies, waits for them, and re-layouts: 1.45 us -> none  [local(): grad_group = jnp.stack([vec[14, :ch], vec[15, :ch]], -1).reshape(2 * ch)]
    unnamed x24 -> x12, local copies, waits for them, and re-layouts: 7.13 us -> 6.83 us
where the time goes in v2:
time: 119 us
  Pallas kernels  111 us (93%)
  local copies, waits for them, and re-layouts  6.83 us (6%)
    pallas_call x1, Pallas kernels, local(): pl.pallas_call(functools.partial(kernel, nd, nt_, T, list(given) + list(r...  107 us
    unnamed x12, local copies, waits for them, and re-layouts  6.83 us
    pallas_call x1, Pallas kernels, local(): pl.pallas_call(functools.partial(writer, list(got) + list(final) + list(h...  4.59 us

profile of v2, /device:TPU:0, one launch (start us, length us, event | category | flops | bytes accessed | tf_op | source)
XLA Modules:
  0.0 119.0 jit_solution(4386676863912060700)
XLA Ops:
  0.7 106.8 %layer.1 = (bf16[512,768]{1,0:T(8,128)(2,1)}, f32[512,768]{1,0:T(8,128)}, bf16[2,8,144,384]{3,2,1,0:T(8,128)(2,1)}, bf16[2,8,48,384]{3,2,1,0:T(8,128)(2,1)}, bf1...) custom-call(bf16[512,768]{1,0:T(8,128)(2,1)} %refs_0_.1, bf16[512,768]{1,0:T(8,128)(2,1)} %refs_1_.1, f32[6,128]{1,0:T(8,128)} %bitcast.35, ...), custom_call_target="tpu_custom_call" | custom-call | tf_op jit(solution)/shard_map/layer/pallas_call | solution.py:933
  107.4 0.0 copy-start
  107.5 1.5 %copy-done = bf16[2,8,144,384]{3,2,1,0:T(8,128)(2,1)S(1)} copy-done((bf16[2,8,144,384]{3,2,1,0:T(8,128)(2,1)S(1)}, bf16[2,8,144,384]{3,2,1,0:T(8,128)(2,1)}, u32[]{:S(2)}) %copy-start) | copy-done | bytes 1769496
  108.9 0.0 copy-start.1
  108.9 1.4 %copy-done.1 = f32[512,768]{1,0:T(8,128)S(1)} copy-done((f32[512,768]{1,0:T(8,128)S(1)}, f32[512,768]{1,0:T(8,128)}, u32[]{:S(2)}) %copy-start.1) | copy-done | bytes 1572888
  110.3 0.0 copy-start.2
  110.3 1.1 copy-done.2
  111.5 0.0 copy-start.3
  111.5 1.1 copy-done.3
  112.5 0.0 copy-start.4
  112.5 1.1 copy-done.4
  113.6 0.0 copy-start.5
  113.6 0.7 copy-done.5
  114.3 4.6 %writer.1 = (bf16[512,768]{1,0:T(8,128)(2,1)}, f32[512,768]{1,0:T(8,128)}, f32[6,128]{1,0:T(8,128)}, f32[4,48,768]{2,1,0:T(8,128)}, f32[2,48,768]{2,1,0:T(8,128)...) custom-call(bf16[512,768]{1,0:T(8,128)(2,1)S(1)} %copy-done.2, ...), custom_call_target="tpu_custom_call" | custom-call | tf_op jit(solution)/shard_map/writer/pallas_call | solution.py:973
Async XLA Ops:
  107.4 1.5 %copy-start = (bf16[2,8,144,384]{3,2,1,0:T(8,128)(2,1)S(1)}, bf16[2,8,144,384]{3,2,1,0:T(8,128)(2,1)}, u32[]{:S(2)}) copy-start(bf16[2,8,144,384]{3,2,1,0:T(8,128)(2,1)} %get-tuple-element.36.refs_2_) | copy-start | bytes 5308420
  108.9 1.4 %copy-start.1 = (f32[512,768]{1,0:T(8,128)S(1)}, f32[512,768]{1,0:T(8,128)}, u32[]{:S(2)}) copy-start(f32[512,768]{1,0:T(8,128)} %get-tuple-element.35.refs_1_) | copy-start | bytes 4718596
  110.3 1.1 copy-start.2
  111.5 1.1 copy-start.3
  112.5 1.1 copy-start.4
  113.6 0.7 copy-start.5

commit v3 on v2

--- a/solution.py
+++ b/solution.py
@@ -12,6 +12,7 @@
 F32 = jnp.float32
 GROUP = 64
 LANES = 128
+SENDS = 56
 
 
 def nn(a, b):
@@ -77,7 +78,6 @@
         PAR=pltpu.VMEM((nt_, 8, LANES), F32),
         WRP=pltpu.VMEM((nt_, 640, 768), BF),
         WXP=pltpu.VMEM((nt_, 256, 768), BF),
-        PERM=pltpu.VMEM((6, T, LANES), F32),
         X=pltpu.VMEM((T, 768), F32),
         GY=pltpu.VMEM((T, 768), BF),
         LOW=pltpu.VMEM((T, 768), BF),
@@ -87,17 +87,14 @@
         BI=pltpu.VMEM((nt_, T, LANES), F32),
         HR=pltpu.VMEM((nt_, T + 8, LANES), F32),
         HI=pltpu.VMEM((nt_, T + 8, LANES), F32),
-        NR=pltpu.VMEM((nt_, T, LANES), F32),
-        NI=pltpu.VMEM((nt_, T, LANES), F32),
+        N2=pltpu.VMEM((max(6, 2 * nt_), T, LANES), F32),
         RS=pltpu.VMEM((nt_, T, LANES), F32),
         MIX=pltpu.VMEM((nt_, T, 256), BF),
         RES=pltpu.VMEM((T, 768), F32),
         MID=pltpu.VMEM((T, 768), BF),
-        COT=pltpu.VMEM((T, 768), BF),
         HID=pltpu.VMEM((nt_, T, 384), BF),
         DG=pltpu.VMEM((nt_, T, 768), BF),
-        NAT=pltpu.VMEM((T, 768), F32),
-        GRES=pltpu.VMEM((T, 768), F32),
+        ACC=pltpu.VMEM((nt_, T, 768), F32),
         CH=pltpu.VMEM((3, nt_ * 8, LANES), F32),
         ST=pltpu.VMEM((2, nt_ * 8, LANES), F32),
         EX0=pltpu.VMEM((nd, 16, LANES), F32),
@@ -109,31 +106,57 @@
         **sum_buffers("SL", nd, 48),
         loc=dma((16,)),
         out=dma((8,)),
-        ss=dma((160,)),
-        rs=dma((160,)),
+        ss=dma((SENDS,)),
+        rs=dma((92 + 6 * max(0, nd.bit_length() - 4),)),
+        fs=dma((8,)),
         es=dma((4, nd)),
         er=dma((4, nd)),
     )
 
 
 class Links:
-    def __init__(self, ss, rs):
-        self.ss, self.rs, self.used, self.open = ss, rs, 0, []
+    def __init__(self, ss, rs, fs):
+        self.ss, self.rs, self.fs = ss, rs, fs
+        self.free, self.received, self.asked = list(range(SENDS)), 0, 0
+        self.open, self.old, self.some = [], [], []
 
     def send(self, src, dst, dev):
-        k = self.used
-        self.used += 1
+        k, n = self.received, self.free.pop(0)
+        self.received += 1
         copy = pltpu.make_async_remote_copy(
-            src, dst, self.ss.at[k], self.rs.at[k], device_id=dev, device_id_type=MESH
+            src, dst, self.ss.at[n], self.rs.at[k], device_id=dev, device_id_type=MESH
         )
         copy.start()
-        self.open.append(copy)
+        self.open.append((copy, n))
         return copy
 
+    def retire(self, copies):
+        self.old += [pair for c in copies for pair in self.open if pair[0] is c]
+        while len(self.old) > 4:
+            pair = self.old.pop(0)
+            pair[0].wait_send()
+            self.free.append(pair[1])
+            self.open = [p for p in self.open if p is not pair]
+
+    def send_if(self, flag, k, src, dst, dev):
+        n = self.asked
+        self.asked += 1
+        copy = pltpu.make_async_remote_copy(
+            src, dst, self.fs.at[n], self.rs.at[k], device_id=dev, device_id_type=MESH
+        )
+
+        @pl.when(flag)
+        def _():
+            copy.start()
+
+        self.some.append((flag, copy))
+        return copy
+
     def drain(self):
-        for copy in self.open:
+        for copy, _ in self.open:
             copy.wait_send()
-        self.open = []
+        for flag, copy in self.some:
+            pl.when(flag)(copy.wait_send)
 
 
 def kernel(nd, nt_, T, names, *refs):
@@ -150,7 +173,7 @@
     order = ((1, 2), (2, 1))
     place = [bits[0] * 4 + bits[f] * 2 + bits[s] for f, s in order]
     wide = [bits[0] * 2 + bits[f] for f, s in order]
-    links = Links(r["ss"], r["rs"])
+    links = Links(r["ss"], r["rs"], r["fs"])
     away = [0, 1, 3, 2] if nt_ == 4 else blocks
 
     def slot(k):
@@ -173,6 +196,7 @@
     lax.fori_loop(1, nd, greet_dp, 0)
 
     WM = r["WM"]
+    COT = r["DG"].at[nt_ - 1]
     loads = {}
     for k, (name, src, dst) in enumerate(
         (
@@ -185,7 +209,7 @@
             ("u", r["wu"], WM.at[1, :, 0, 0:96, :]),
             ("d0", r["wd"].at[:, :, 0:384], WM.at[0, :, 0, 96:144, :]),
             ("d1", r["wd"].at[:, :, 384:768], WM.at[1, :, 0, 96:144, :]),
-            ("cot", r["cot"], r["COT"]),
+            ("cot", r["cot"], COT),
         )
     ):
         loads[name] = pltpu.make_async_copy(src, dst, r["loc"].at[k])
@@ -224,26 +248,47 @@
         return (flip(1 << b), z)
 
     class Unit:
-        def __init__(self, buf, slots, portions):
-            self.buf, self.slots, self.portions = buf, slots, portions
+        def __init__(self, buf, slots, portions, far=None):
+            self.buf, self.slots, self.portions, self.far = buf, slots, portions, far
+            self.at = place if portions == 8 else wide
             self.todo = []
 
         def wait(self):
             for copy in self.todo:
                 copy.wait_recv()
+            links.retire(self.todo)
             self.todo = []
 
         def hop(self, h, b, start, count):
             part = self.buf.at[h, pl.ds(start, count), pl.ds(self.slots[0], len(self.slots))]
             self.todo.append(links.send(part, part, partner(b)))
 
+        def held(self, h, s):
+            if self.far is None:
+                return self.buf.at[h, self.at[h], s]
+            return self.buf.at[h, pl.ds(bits[0] * 4 + bits[order[h][0]] * 2, 2), s]
+
         def z(self):
             for s in self.slots:
                 for h in range(2):
-                    at = place[h] if self.portions == 8 else wide[h]
-                    self.todo.append(
-                        links.send(self.buf.at[h, at, 0], self.buf.at[h, at, s], across(away[s]))
-                    )
+                    own, to = self.held(h, 0), self.held(h, s)
+                    if self.far is None or nt_ != 4:
+                        self.todo.append(links.send(own, to, across(away[s])))
+                    else:
+                        k = links.received
+                        links.received += 1
+                        flag = z != (0 if s == 1 else 3)
+                        self.todo.append(links.send_if(flag, k, own, to, across(away[s])))
+                        self.first = k - h
+
+        def forward(self):
+            if nt_ != 4:
+                return
+            s = self.slots[0]
+            who, end = (2, 3) if s == 1 else (1, 0)
+            for h in range(2):
+                held, to = self.held(h, self.far), self.held(h, s)
+                links.send_if(z == who, self.first + h, held, to, (me, end))
 
         def s(self):
             self.wait()
@@ -268,13 +313,13 @@
 
     I1, I2 = Unit(WI, blocks[1:3], 8), Unit(WI, blocks[3:], 8)
     XM = Unit(WX, blocks[1:], 4)
-    M1, M2, M3 = [Unit(WM, [s], 8) for s in blocks[1:]]
+    M1, M2, M3 = Unit(WM, [1], 8, 3), Unit(WM, [2], 8, 3), Unit(WM, [3], 8)
 
     pl.semaphore_wait(barrier, nd - 1 + nt_ - 1)
     I1.z()
     par_copies = [links.send(PAR.at[0], PAR.at[s], across(away[s])) for s in blocks[1:]]
 
-    PERM, X, GY, LOW = r["PERM"], r["X"], r["GY"], r["LOW"]
+    PERM, X, GY, LOW = r["N2"], r["X"], r["GY"], r["LOW"]
     loads["tokens"].wait()
     tiles = [slice(LANES * i, LANES * i + LANES) for i in range(6)]
     for i in range(6):
@@ -304,6 +349,9 @@
 
     norm_rows(X, gain1, LOW)
     I2.z()
+    for k in ("g", "u", "d0", "d1", "cot"):
+        loads[k].wait()
+    M3.z()
 
     for k in blocks:
         for g in range(5):
@@ -345,16 +393,14 @@
             WX[h, p, 0] = mixed_rows[48 * p : 48 * p + 48, 384 * h : 384 * h + 384]
     spread_mix(0)
     I1.s()
-    XM.z()
     project(0)
-    for k in ("g", "u", "d0", "d1", "cot"):
-        loads[k].wait()
     I1.f()
+    M1.z()
+    M2.z()
     I2.s()
-    M1.z()
 
     for i in range(6):
-        PERM[i] = r["COT"][:, tiles[i]].astype(F32)
+        PERM[i] = COT[:, tiles[i]].astype(F32)
 
     def take_cot(k, c):
         for i in range(6):
@@ -363,21 +409,20 @@
         return c
 
     lax.fori_loop(0, steps // 2, take_cot, 0, unroll=2)
+    I1.c()
     I2.f()
-    I1.c()
-    XM.s()
-    M2.z()
+    XM.z()
     for copy in par_copies:
         copy.wait_recv()
     I1.wait()
     lax.fori_loop(1, 3, lambda k, c: (project(k), c)[1], 0)
+    M3.s()
     I2.c()
-    M1.s()
-    M3.z()
-    XM.c()
     I2.wait()
     project(3)
-    M1.f()
+    M3.f()
+    M1.forward()
+    M2.forward()
 
     CH, ST, HR, HI = r["CH"], r["ST"], r["HR"], r["HI"]
     turn = []
@@ -478,9 +523,7 @@
         return lax.fori_loop(0, nd, lap, (zero4, zero4))
 
     post(r["EX0"], 0, *chain(zero4, zero4, 1.0, False))
-    XM.wait()
-    lax.fori_loop(1, nt_, lambda k, c: (spread_mix(k), c)[1], 0)
-    M2.s()
+    XM.s()
     start = carried(r["EX0"], 0, 1.0)
     chain(start[0], start[1], 1.0, True)
     for k in blocks:
@@ -504,8 +547,10 @@
         return ST[0, 8 * k : 8 * k + 8, :], ST[1, 8 * k : 8 * k + 8, :]
 
     lax.fori_loop(0, steps, states, tuple(held(k) for k in blocks), unroll=4)
-    M1.c()
+    M3.c()
+    M1.f()
     M2.f()
+    XM.c()
 
     half = GROUP // 2
     same = one_hot(cells((LANES, LANES), 0) // half == cells((LANES, LANES), 1) // half)
@@ -515,7 +560,8 @@
         rest = (v - top.astype(F32)).astype(BF)
         return (nn(top, same) + nn(rest, same)) * (1.0 / GROUP)
 
-    NR, NI, RS, MIX = r["NR"], r["NI"], r["RS"], r["MIX"]
+    NR, NI = r["N2"].at[pl.ds(0, nt_)], r["N2"].at[pl.ds(nt_, nt_)]
+    RS, MIX = r["RS"], r["MIX"]
 
     def normalise(k, c):
         hr, hi = HR[k, pl.ds(8, T), :], HI[k, pl.ds(8, T), :]
@@ -532,7 +578,8 @@
         return c
 
     lax.fori_loop(0, nt_, normalise, 0)
-    M3.s()
+    XM.wait()
+    lax.fori_loop(1, nt_, lambda k, c: (spread_mix(k), c)[1], 0)
 
     RES, MID = r["RES"], r["MID"]
     RES[...] = X[...]
@@ -543,8 +590,8 @@
 
     lax.fori_loop(0, nt_, mix_in, 0)
     norm_rows(RES, gain2, MID)
+    M1.c()
     M2.c()
-    M3.f()
 
     HID, DG = r["HID"], r["DG"]
 
@@ -588,6 +635,7 @@
         def stage(self, n):
             for copy in self.todo:
                 copy.wait_recv()
+            links.retire(self.todo)
             self.todo = []
             S = self.bufs[0]
             for h in range(2):
@@ -602,8 +650,9 @@
                     for b in range(3, nd.bit_length() - 1):
                         land = self.further.at[h, pl.ds(b - 3, 1)]
                         one = links.send(S.at[h, part], land, partner(b))
-                        one.wait()
-                        links.open = [c for c in links.open if c is not one]
+                        one.wait_recv()
+                        one.wait_send()
+                        links.free.append(links.open.pop()[1])
                         S[h, part] = (
                             S[h, part].astype(F32) + self.further[h, b - 3 : b - 2].astype(F32)
                         ).astype(BF)
@@ -630,32 +679,33 @@
         copy.start()
         finals.append(copy)
 
+    ACC = r["ACC"]
+    NAT, GRES = ACC.at[0], ACC.at[1]
+
+    def back_mid(k):
+        ACC[k] = nt(DG[k, :, 0:384], gate_w(k, 0)) + nt(DG[k, :, 384:768], gate_w(k, 1))
+
     mlp_sum, early_sum, late_sum = Summed("SM"), Summed("SE"), Summed("SL")
     mlp_sum.stage(0)
+    back_mid(0)
+    M3.wait()
+    swiglu(3)
+    back_mid(3)
+    mlp_sum.stage(1)
     M1.wait()
     swiglu(1)
-    M3.c()
-    mlp_sum.stage(1)
+    back_mid(1)
     M2.wait()
     swiglu(2)
-    M3.wait()
-    swiglu(3)
-
-    GRES, NAT = r["GRES"], r["NAT"]
-    NAT[...] = jnp.zeros((T, 768), F32)
-
-    def back_mid(k, c):
-        j = slot(k)
-        NAT[...] += nt(DG[j, :, 0:384], gate_w(j, 0)) + nt(DG[j, :, 384:768], gate_w(j, 1))
-        return c
-
-    lax.fori_loop(0, nt_, back_mid, 0)
-    mlp_sum.stage(2)
+    back_mid(2)
+
     LOWR = r["MID"]
 
     def back_second(i, total):
         at = pl.ds(pl.multiple_of(i * 128, 128), 128)
-        res, gmid = RES[at, :], NAT[at, :]
+        res, gmid = RES[at, :], ACC[slot(0), at, :]
+        for k in blocks[1:]:
+            gmid = gmid + ACC[slot(k), at, :]
         q2 = lax.rsqrt(jnp.mean(res * res, -1, keepdims=True) + 1e-06)
         p = gmid * gain2
         back = q2 * p - res * (q2 * q2 * q2) * jnp.mean(p * res, -1, keepdims=True)
@@ -751,7 +801,6 @@
 
     back_norm(0, True)
     back_ends([0], r["EX1"], 1)
-    mlp_sum.stage(3)
 
     SE, SL = r["SE"], r["SL"]
     gate_cols = nn(G[0, :, 384:640], together)[:, 0 : 2 * ch].astype(BF)
@@ -761,9 +810,11 @@
         SE[h, 0:4] = tn(gate_cols, LOW[:, at]).astype(BF).reshape(4, 48, 384)
         SE[h, 4:8] = tn(mix_cols, LOWR[:, at]).astype(BF).reshape(4, 48, 384)
     early_sum.stage(0)
+    mlp_sum.stage(2)
     lax.fori_loop(1, nt_, lambda k, c: (back_norm(k, False), c)[1], 0)
-    mlp_sum.stage(4)
     early_sum.stage(1)
+    back_ends(blocks[1:], r["EX2"], 2)
+    mlp_sum.stage(3)
     back_states([0], r["EX1"], 1)
     back_gates(0, True)
     rows, cols = cells((384, 384), 0), cells((384, 384), 1)
@@ -774,37 +825,25 @@
         SL[h] = tn(late_cols, LOW[:, 384 * h : 384 * h + 384]).astype(BF).reshape(8, 48, 384)
     late_sum.stage(0)
     early_sum.stage(2)
-
-    back_ends(blocks[1:], r["EX2"], 2)
+    mlp_sum.stage(4)
+
+    back_states(blocks[1:], r["EX2"], 2)
     late_sum.stage(1)
-    mlp_sum.stage(5)
-    early_sum.stage(3)
-
-    def down(k, c):
-        j = slot(k)
-        for h in range(2):
-            RES[:, 384 * h : 384 * h + 384] += nn(HID[j], down_w(j, h))
-        return c
-
-    lax.fori_loop(0, nt_, down, 0)
-    late_sum.stage(2)
-    early_sum.stage(4)
-    back_states(blocks[1:], r["EX2"], 2)
-    late_sum.stage(3)
     for k in blocks[1:]:
         back_gates(k, False)
-    early_sum.stage(5)
-    late_sum.stage(4)
-    mlp_sum.stage(6)
-    put_out(r["SMF"], r["o_mlp"])
-
-    NAT[...] = jnp.zeros((T, 768), F32)
+    early_sum.stage(3)
+    late_sum.stage(2)
+    mlp_sum.stage(5)
 
     def back_in(k, c):
         NAT[...] += nn(G[slot(k), :, 0:640], WRP[slot(k)])
         return c
 
-    lax.fori_loop(0, nt_, back_in, 0)
+    NAT[...] = nn(G[slot(0), :, 0:640], WRP[slot(0)])
+    lax.fori_loop(1, nt_ // 2, back_in, 0)
+    late_sum.stage(3)
+    lax.fori_loop(nt_ // 2, nt_, back_in, 0)
+    early_sum.stage(4)
 
     def back_first(i, total):
         at = pl.ds(pl.multiple_of(i * 128, 128), 128)
@@ -818,9 +857,7 @@
     for i in range(6):
         VEC[me, i : i + 1, :] = gnorm1[:, 128 * i : 128 * i + 128]
     exchange(3, VEC, "go")
-    late_sum.stage(5)
-    early_sum.stage(6)
-    put_out(r["SEF"], r["o_early"])
+    late_sum.stage(4)
 
     def put_from(buf):
         def put(k, c):
@@ -834,12 +871,26 @@
     for i in range(6):
         NAT[:, tiles[i]] = PERM[i]
     put_out(NAT, r["tok"])
+    mlp_sum.stage(6)
+    put_out(r["SMF"], r["o_mlp"])
+
+    def down(k, c):
+        j = slot(k)
+        for h in range(2):
+            RES[:, 384 * h : 384 * h + 384] += nn(HID[j], down_w(j, h))
+        return c
+
+    lax.fori_loop(0, nt_, down, 0)
+    late_sum.stage(5)
+    early_sum.stage(5)
     put_from(RES)
     for i in range(6):
-        r["COT"][:, tiles[i]] = PERM[i].astype(BF)
-    put_out(r["COT"], r["mixed"])
+        COT[:, tiles[i]] = PERM[i].astype(BF)
+    put_out(COT, r["mixed"])
     late_sum.stage(6)
     put_out(r["SLF"], r["o_late"])
+    early_sum.stage(6)
+    put_out(r["SEF"], r["o_early"])
 
     exchange(3, VEC, "arrive")
     total = VEC[0]
@@ -864,12 +915,36 @@
         c.start()
         return c
 
-    ins = {
-        "late": copy(r["late"], r["L"]),
-        "early": copy(r["early"], r["E"]),
-        "mlp": copy(r["mlp"], r["M"]),
-    }
-    outs = [copy(r["mixed_in"], r["mixed"]), copy(r["tok_in"], r["tok"])]
+    ins = {}
+    for name, src, dst in (
+        ("tok", "tok_in", "TK"),
+        ("mlp", "mlp", "M"),
+        ("mixed", "mixed_in", "MX"),
+        ("early", "early", "E"),
+        ("late", "late", "L"),
+    ):
+        ins[name] = copy(r[src], r[dst])
+    outs = []
+    ins["tok"].wait()
+    outs.append(copy(r["TK"], r["tok"]))
+    ins["mlp"].wait()
+    for h, name in ((0, "g_g"), (1, "g_u")):
+        r["GF"][h] = r["M"][h, :, 0:96, :].astype(F32)
+        outs.append(copy(r["GF"].at[h], r[name]))
+    ins["mixed"].wait()
+    outs.append(copy(r["MX"], r["mixed"]))
+    for h in range(2):
+        r["DF"][:, :, 384 * h : 384 * h + 384] = r["M"][h, :, 96:144, :].astype(F32)
+    outs.append(copy(r["DF"], r["g_d"]))
+    for name, a, f, n, dests in (
+        ("early", "E", "EF", 8, (("g_o", 0, 4), ("g_x", 4, 8))),
+        ("late", "L", "LF", 6, (("g_in", 0, 4), ("g_f", 4, 6))),
+    ):
+        ins[name].wait()
+        for h in range(2):
+            r[f][:, :, 384 * h : 384 * h + 384] = r[a][h, 0:n].astype(F32)
+        for dst, p, q in dests:
+            outs.append(copy(r[f].at[p:q], r[dst]))
     ch = r["gap"].shape[1]
     vec = r["vec"]
     r["gn1"][...] = vec[0:6, :]
@@ -877,22 +952,6 @@
     r["gap"][...] = vec[12:13, 0:ch]
     r["phase"][...] = vec[13:14, 0:ch]
     r["group"][...] = jnp.concatenate([vec[14:15, :], vec[15:16, 0 : 2 * ch - LANES]], axis=1)
-    for name, a, outs_of in (
-        ("late", "L", (("LF", 0, 6, (("g_in", 0, 4), ("g_f", 4, 6))),)),
-        ("early", "E", (("EF", 0, 8, (("g_o", 0, 4), ("g_x", 4, 8))),)),
-    ):
-        ins[name].wait()
-        for f, lo, hi, dests in outs_of:
-            for h in range(2):
-                r[f][lo:hi, :, 384 * h : 384 * h + 384] = r[a][h, lo:hi].astype(F32)
-            for dst, p, q in dests:
-                outs.append(copy(r[f].at[p:q], r[dst]))
-    ins["mlp"].wait()
-    for h, name in ((0, "g_g"), (1, "g_u")):
-        r["GF"][h] = r["M"][h, :, 0:96, :].astype(F32)
-        outs.append(copy(r["GF"].at[h], r[name]))
-        r["DF"][:, :, 384 * h : 384 * h + 384] = r["M"][h, :, 96:144, :].astype(F32)
-    outs.append(copy(r["DF"], r["g_d"]))
     for c in outs:
         c.wait()
 
@@ -963,11 +1022,13 @@
         L=pltpu.VMEM((2, 8, 48, 384), BF),
         E=pltpu.VMEM((2, 8, 48, 384), BF),
         M=pltpu.VMEM((2, 8, 144, 384), BF),
+        MX=pltpu.VMEM((T, D), BF),
+        TK=pltpu.VMEM((T, D), F32),
         LF=pltpu.VMEM((6, 48, D), F32),
         EF=pltpu.VMEM((8, 48, D), F32),
         GF=pltpu.VMEM((2, 8, 96, 384), F32),
         DF=pltpu.VMEM((8, 48, D), F32),
-        sem=pltpu.SemaphoreType.DMA((16,)),
+        sem=pltpu.SemaphoreType.DMA((15,)),
     )
     blocky = ("gn1", "gn2", "gap", "phase", "group")
     outs = pl.pallas_call(
@@ -976,7 +1037,7 @@
         in_specs=[vmem if k == "vec" else hbm for k in got],
         out_specs=[vmem if k in blocky else hbm for k in final],
         scratch_shapes=list(held.values()),
-        compiler_params=pltpu.CompilerParams(vmem_limit_bytes=32 * 2**20),
+        compiler_params=pltpu.CompilerParams(vmem_limit_bytes=62 * 2**20),
         name="writer",
     )(*got.values())
     o = dict(zip(final, outs))

time: 119 us -> 112 us (0.941)
  local copies, waits for them, and re-layouts: 6.83 us -> 0 us
    unnamed x12 -> x0, local copies, waits for them, and re-layouts: 6.83 us -> none
    pallas_call x1, Pallas kernels: 107 us -> 105 us  [local(): pl.pallas_call(functools.partial(kernel, nd, nt_, T, list(given) + list(r...]
    pallas_call x1, Pallas kernels: 4.59 us -> 6.11 us  [local(): pl.pallas_call(functools.partial(writer, list(got) + list(final) + list(h...]
where the time goes in v3:
time: 112 us
  Pallas kernels  111 us (99%)
    pallas_call x1, Pallas kernels, local(): pl.pallas_call(functools.partial(kernel, nd, nt_, T, list(given) + list(r...  105 us
    pallas_call x1, Pallas kernels, local(): pl.pallas_call(functools.partial(writer, list(got) + list(final) + list(h...  6.11 us

profile of v3, /device:TPU:0, one launch (start us, length us, event | category | flops | bytes accessed | tf_op | source)
XLA Modules:
  0.0 112.1 jit_solution(9123601275871652465)
XLA Ops:
  0.7 105.1 %layer.1 = (bf16[512,768]{1,0:T(8,128)(2,1)}, f32[512,768]{1,0:T(8,128)}, bf16[2,8,144,384]{3,2,1,0:T(8,128)(2,1)}, bf16[2,8,48,384]{3,2,1,0:T(8,128)(2,1)}, bf1...) custom-call(bf16[512,768]{1,0:T(8,128)(2,1)} %refs_0_.1, bf16[512,768]{1,0:T(8,128)(2,1)} %refs_1_.1, f32[6,128]{1,0:T(8,128)} %bitcast.35, ...), custom_call_target="tpu_custom_call" | custom-call | tf_op jit(solution)/shard_map/layer/pallas_call | solution.py:992
  105.8 6.1 %writer.1 = (bf16[512,768]{1,0:T(8,128)(2,1)}, f32[512,768]{1,0:T(8,128)}, f32[6,128]{1,0:T(8,128)}, f32[4,48,768]{2,1,0:T(8,128)}, f32[2,48,768]{2,1,0:T(8,128)...) custom-call(bf16[512,768]{1,0:T(8,128)(2,1)} %get-tuple-element.34.r, ...), custom_call_target="tpu_custom_call" | custom-call | tf_op jit(solution)/shard_map/writer/pallas_call | solution.py:1034

commit v4 on v3

--- a/solution.py
+++ b/solution.py
@@ -582,16 +582,17 @@
     lax.fori_loop(1, nt_, lambda k, c: (spread_mix(k), c)[1], 0)
 
     RES, MID = r["RES"], r["MID"]
-    RES[...] = X[...]
-
-    def mix_in(k, c):
-        RES[...] += nn(MIX[slot(k)], WXP[slot(k)])
+
+    def mix_in(i, c):
+        at = pl.ds(pl.multiple_of(i * 256, 256), 256)
+        total = nn(MIX[slot(0), at, :], WXP[slot(0)])
+        for k in blocks[1:]:
+            total = total + nn(MIX[slot(k), at, :], WXP[slot(k)])
+        RES[at, :] = X[at, :] + total
         return c
 
-    lax.fori_loop(0, nt_, mix_in, 0)
+    lax.fori_loop(0, T // 256, mix_in, 0)
     norm_rows(RES, gain2, MID)
-    M1.c()
-    M2.c()
 
     HID, DG = r["HID"], r["DG"]
 
@@ -688,11 +689,13 @@
     mlp_sum, early_sum, late_sum = Summed("SM"), Summed("SE"), Summed("SL")
     mlp_sum.stage(0)
     back_mid(0)
+    M1.c()
+    M2.c()
     M3.wait()
     swiglu(3)
     back_mid(3)
+    M1.wait()
     mlp_sum.stage(1)
-    M1.wait()
     swiglu(1)
     back_mid(1)
     M2.wait()
@@ -814,7 +817,6 @@
     lax.fori_loop(1, nt_, lambda k, c: (back_norm(k, False), c)[1], 0)
     early_sum.stage(1)
     back_ends(blocks[1:], r["EX2"], 2)
-    mlp_sum.stage(3)
     back_states([0], r["EX1"], 1)
     back_gates(0, True)
     rows, cols = cells((384, 384), 0), cells((384, 384), 1)
@@ -824,16 +826,16 @@
     for h in range(2):
         SL[h] = tn(late_cols, LOW[:, 384 * h : 384 * h + 384]).astype(BF).reshape(8, 48, 384)
     late_sum.stage(0)
+    mlp_sum.stage(3)
+
+    back_states(blocks[1:], r["EX2"], 2)
+    late_sum.stage(1)
     early_sum.stage(2)
     mlp_sum.stage(4)
-
-    back_states(blocks[1:], r["EX2"], 2)
-    late_sum.stage(1)
     for k in blocks[1:]:
         back_gates(k, False)
     early_sum.stage(3)
     late_sum.stage(2)
-    mlp_sum.stage(5)
 
     def back_in(k, c):
         NAT[...] += nn(G[slot(k), :, 0:640], WRP[slot(k)])
@@ -843,6 +845,7 @@
     lax.fori_loop(1, nt_ // 2, back_in, 0)
     late_sum.stage(3)
     lax.fori_loop(nt_ // 2, nt_, back_in, 0)
+    mlp_sum.stage(5)
     early_sum.stage(4)
 
     def back_first(i, total):

time: 112 us -> 107 us (0.955)
  Pallas kernels: 111 us -> 105 us
    pallas_call x1, Pallas kernels: 105 us -> 99.3 us  [local(): pl.pallas_call(functools.partial(kernel, nd, nt_, T, list(given) + list(r...]
where the time goes in v4:
time: 107 us; the launch traced here: 106 us
  Pallas kernels  105 us (98%)
    pallas_call x1, Pallas kernels, local(): pl.pallas_call(functools.partial(kernel, nd, nt_, T, list(given) + list(r...  99.3 us
    pallas_call x1, Pallas kernels, local(): pl.pallas_call(functools.partial(writer, list(got) + list(final) + list(h...  6.11 us

profile of v4, /device:TPU:0, one launch (start us, length us, event | category | flops | bytes accessed | tf_op | source)
XLA Modules:
  0.0 106.3 jit_solution(7246992033903110359)
XLA Ops:
  0.7 99.3 %layer.1 = (bf16[512,768]{1,0:T(8,128)(2,1)}, f32[512,768]{1,0:T(8,128)}, bf16[2,8,144,384]{3,2,1,0:T(8,128)(2,1)}, bf16[2,8,48,384]{3,2,1,0:T(8,128)(2,1)}, bf1...) custom-call(bf16[512,768]{1,0:T(8,128)(2,1)} %refs_0_.1, bf16[512,768]{1,0:T(8,128)(2,1)} %refs_1_.1, f32[6,128]{1,0:T(8,128)} %bitcast.35, ...), custom_call_target="tpu_custom_call" | custom-call | tf_op jit(solution)/shard_map/layer/pallas_call | solution.py:995
  100.0 6.1 %writer.1 = (bf16[512,768]{1,0:T(8,128)(2,1)}, f32[512,768]{1,0:T(8,128)}, f32[6,128]{1,0:T(8,128)}, f32[4,48,768]{2,1,0:T(8,128)}, f32[2,48,768]{2,1,0:T(8,128)...) custom-call(bf16[512,768]{1,0:T(8,128)(2,1)} %get-tuple-element.34.r, ...), custom_call_target="tpu_custom_call" | custom-call | tf_op jit(solution)/shard_map/writer/pallas_call | solution.py:1037

commit v5 on v4

--- a/solution.py
+++ b/solution.py
@@ -12,7 +12,7 @@
 F32 = jnp.float32
 GROUP = 64
 LANES = 128
-SENDS = 56
+SENDS = 40
 
 
 def nn(a, b):
@@ -104,8 +104,8 @@
         **sum_buffers("SM", nd, 144),
         **sum_buffers("SE", nd, 48),
         **sum_buffers("SL", nd, 48),
-        loc=dma((16,)),
-        out=dma((8,)),
+        loc=dma((10,)),
+        out=dma((5,)),
         ss=dma((SENDS,)),
         rs=dma((92 + 6 * max(0, nd.bit_length() - 4),)),
         fs=dma((8,)),

time: 107 us -> 106 us (level)
  no operation moved by 1% of the time
where the time goes in v5:
time: 106 us
  Pallas kernels  105 us (99%)
    pallas_call x1, Pallas kernels, local(): pl.pallas_call(functools.partial(kernel, nd, nt_, T, list(given) + list(r...  99.1 us
    pallas_call x1, Pallas kernels, local(): pl.pallas_call(functools.partial(writer, list(got) + list(final) + list(h...  6.11 us

profile of v5, /device:TPU:0, one launch (start us, length us, event | category | flops | bytes accessed | tf_op | source)
XLA Modules:
  0.0 106.0 jit_solution(16405525976228025969)
XLA Ops:
  0.7 99.1 %layer.1 = (bf16[512,768]{1,0:T(8,128)(2,1)}, f32[512,768]{1,0:T(8,128)}, bf16[2,8,144,384]{3,2,1,0:T(8,128)(2,1)}, bf16[2,8,48,384]{3,2,1,0:T(8,128)(2,1)}, bf1...) custom-call(bf16[512,768]{1,0:T(8,128)(2,1)} %refs_0_.1, bf16[512,768]{1,0:T(8,128)(2,1)} %refs_1_.1, f32[6,128]{1,0:T(8,128)} %bitcast.35, ...), custom_call_target="tpu_custom_call" | custom-call | tf_op jit(solution)/shard_map/layer/pallas_call | solution.py:995
  99.8 6.1 %writer.1 = (bf16[512,768]{1,0:T(8,128)(2,1)}, f32[512,768]{1,0:T(8,128)}, f32[6,128]{1,0:T(8,128)}, f32[4,48,768]{2,1,0:T(8,128)}, f32[2,48,768]{2,1,0:T(8,128)...) custom-call(bf16[512,768]{1,0:T(8,128)(2,1)} %get-tuple-element.34.r, ...), custom_call_target="tpu_custom_call" | custom-call | tf_op jit(solution)/shard_map/writer/pallas_call | solution.py:1037
